TPU v7x, 256 devices: a whole 4x4x8 slice. The times are simulated.
256 devices in a mesh: prow: 32 (over z_hi, x, y), pcol: 8 (over z_lo, core).
Axes of the slice: x: 4, y: 4, z: 8 (z_hi: 2, z_lo: 4; z = z_hi * 4 + z_lo), core: 2. Of those that a mesh axis runs over, the one named last changes fastest.
Arguments:
- ancestor_inverse: bfloat16 [20480, 20480], P('prow', 'pcol'), may hold values from -6 to 6
- lower_panel: bfloat16 [2, 20480, 512], P(None, 'pcol'), may hold values from -0.0625 to 0.0625
- pattern: int32 [2, 80], replicated, may hold values from 0 to 159, as said below
- diag_inverse: float32 [2, 512, 512], P(None, ('prow', 'pcol')), may hold values from -6 to 6
Outputs:
- off_diagonal: bfloat16 [2, 20480, 512], P(None, ('prow', 'pcol'))
- diagonal_block: float32 [2, 512, 512], P(None, ('prow', 'pcol'))
Inputs may be any that keep to these rules, and one draw needn't show every extreme that they name: `pattern`: each row lists 80 distinct block indices in increasing order, the first 0 and the last 159.
All inputs are finite; a program needn't handle non-finite values.
Results may differ from a plain program's by a relative error of at most 0.0095.
Values may be sent and summed in bfloat16 or wider, within the bound.
No kernel may reach another device: no remote copies, remote signals or barrier semaphores. Data moves between devices by JAX's collectives and lax.ppermute only.
A program may use at most 64 MiB of HBM per device.

v0:
```python
import jax
import jax.numpy as jnp
from jax import lax
from jax.sharding import PartitionSpec as P

BLOCK = 128


def local(ancestor_inverse, lower_panel, pattern, diag_inverse):
    prow_count = lax.axis_size("prow")
    pcol_count = lax.axis_size("pcol")
    row_place = lax.axis_index("prow")
    col_place = lax.axis_index("pcol")
    height, breadth = ancestor_inverse.shape
    column_ids = (col_place * breadth + jnp.arange(breadth, dtype=jnp.int32)) // BLOCK
    column_mask = jnp.any(pattern[:, :, None] == column_ids[None, None, :], axis=1)
    masked = lower_panel * column_mask[:, :, None].astype(lower_panel.dtype)
    share = height // pcol_count
    joined = jnp.concatenate([masked[0], masked[1]], axis=1)
    summed = lax.psum_scatter(
        jnp.dot(ancestor_inverse, joined, preferred_element_type=jnp.float32),
        "pcol",
        scatter_dimension=0,
        tiled=True,
    )
    wide = lower_panel.shape[2]
    product_pair = jnp.stack([summed[:, :wide], summed[:, wide:]])
    row_ids = (row_place * height + col_place * share + jnp.arange(share, dtype=jnp.int32)) // BLOCK
    row_mask = jnp.any(pattern[:, :, None] == row_ids[None, None, :], axis=1)
    off_diagonal = (-(product_pair * row_mask[:, :, None].astype(jnp.float32))).astype(jnp.bfloat16)
    group = prow_count // pcol_count
    owner = row_place // group
    offset = row_place % group * height
    own_rows = lax.dynamic_slice_in_dim(masked, offset, height, 1)
    contribution = jnp.where(col_place == owner, own_rows.astype(jnp.float32), 0.0)
    mine = lax.psum_scatter(
        contribution.astype(jnp.bfloat16), "pcol", scatter_dimension=1, tiled=True
    )
    partial_sum = jnp.einsum(
        "sna,snb->sab", mine.astype(jnp.float32), product_pair, precision=lax.Precision.HIGHEST
    )
    reduced = lax.psum_scatter(partial_sum, ("prow", "pcol"), scatter_dimension=1, tiled=True)
    return (off_diagonal, diag_inverse + reduced)


def solution(mesh):
    placed = (P("prow", "pcol"), P(None, "pcol", None), P(), P(None, ("prow", "pcol"), None))
    return jax.shard_map(
        local,
        mesh=mesh,
        in_specs=placed,
        out_specs=(P(None, ("prow", "pcol"), None), P(None, ("prow", "pcol"), None)),
        check_vma=False,
    )
```

profile of v0, /device:TPU:1, one launch (start us, length us, event | category | flops | bytes accessed | tf_op | source)
XLA Modules:
  0.0 382.5 jit_solution(5907988335303006890)
XLA Ops:
  7.2 0.0 copy-start
  7.2 0.0 reduce-scatter.8.cloned.1.call-start
  7.2 1.1 compare_reduce_fusion
  8.4 3.9 %broadcast_multiply_fusion = bf16[2,2560,512]{2,1,0:T(8,128)(2,1)S(1)} fusion(bf16[2,2560,512]{2,1,0:T(8,128)(2,1)} %param.5, bf16[2,2560]{1,0:T(2,128)(2,1)S(1)} %convert_element_type.26), kind=kLoop, calls=%fused_computation.7 | loop fusion | flops 2621440 | bytes 10496000 | tf_op jit(solution)/shard_map/mul | solution.py:17
  12.4 0.3 slice_bitcast_fusion.1
  12.7 1.9 copy-done.1
  14.7 5.8 %fusion.4 = f32[640,1024]{0,1:T(8,128)} fusion(bf16[640,2560]{1,0:T(8,128)(2,1)S(1)} %copy-done, bf16[2560,512]{1,0:T(8,128)(2,1)S(1)} %get-tuple-element.5, bf16[2560,512]{1,0:T(8,128)(2,1)S(1)} %get-tuple-element.4), kind=kOutput, calls=%fused_computation.8 | convolution fusion | flops 3365928960 | bytes 11141120 | tf_op jit(solution)/shard_map/dot_general | solution.py:21
  20.5 3.3 copy.12
  23.7 0.0 reduce-scatter.8.cloned.1.call-update
  23.8 0.0 reduce-scatter.6.cloned.1.call-start
  23.8 2.7 select_convert_fusion
  26.6 0.0 reduce-scatter.6.cloned.1.call-update
  26.6 0.0 copy-start.3
  26.6 0.0 all-reduce.3.cloned.1.call-start
  26.6 41.3 %reduce-scatter.8.cloned.1.call-done = f32[80,1024]{1,0:T(8,128)} async-done(((f32[640,1024]{1,0:T(8,128)}), f32[80,1024]{1,0:T(8,128)}) %reduce-scatter.8.cloned.1.call-update) | async-done | bytes 327696 | tf_op jit(solution)/shard_map/reduce_scatter | solution.py:20
  68.0 1.7 slice_bitcast_fusion.3
  69.6 38.2 %reduce-scatter.6.cloned.1.call-done = bf16[2,80,512]{2,1,0:T(8,128)(2,1)} async-done(((bf16[2,640,512]{2,1,0:T(8,128)(2,1)}), bf16[2,80,512]{2,1,0:T(8,128)(2,1)}) %reduce-scatter.6.cloned.1.call-update) | async-done | bytes 163856 | tf_op jit(solution)/shard_map/reduce_scatter | solution.py:36
  107.8 3.4 fusion.7
  111.1 0.0 all-reduce.3.cloned.1.call-update
  111.2 0.1 compare_reduce_fusion.1
  111.3 1.7 negate_convert_fusion
  113.0 261.6 %all-reduce.3.cloned.1.call-done = f32[2,512,512]{2,1,0:T(8,128)} async-done(((f32[2,512,512]{2,1,0:T(8,128)}), f32[2,512,512]{2,1,0:T(8,128)}) %all-reduce.3.cloned.1.call-update) | async-done | bytes 2097168
  374.6 0.0 copy-done.2
  374.7 1.4 dynamic-slice_add_fusion
  (8 shorter events, 0.1 us)
Async XLA Ops:
  7.2 7.5 %copy-start = (bf16[640,2560]{1,0:T(8,128)(2,1)S(1)}, bf16[640,2560]{1,0:T(8,128)(2,1)}, u32[]{:S(2)}) copy-start(bf16[640,2560]{1,0:T(8,128)(2,1)} %param.4) | copy-start | bytes 9830404
  7.2 60.8 %reduce-scatter.8.cloned.1.call-start = ((), (), s32[]{:S(2)}) async-start(), calls=%async_computation.3 | async-start | bytes 2949120 | tf_op jit(solution)/shard_map/reduce_scatter | solution.py:20
  12.3 2.3 copy-start.1
  23.8 84.0 %reduce-scatter.6.cloned.1.call-start = ((), (), s32[]{:S(2)}) async-start(), calls=%async_computation.2 | async-start | bytes 1474560 | tf_op jit(solution)/shard_map/reduce_scatter | solution.py:36
  26.6 84.6 %copy-start.3 = (s32[2,80]{1,0:T(2,128)S(1)}, s32[2,80]{1,0:T(2,128)}, u32[]{:S(2)}) copy-start(s32[2,80]{1,0:T(2,128)} %param.6) | copy-start | bytes 1924
  26.6 348.1 %all-reduce.3.cloned.1.call-start = ((), (), s32[]{:S(2)}) async-start(), calls=%async_computation.4 | async-start | bytes 4194304
  69.6 305.0 %copy-start.2 = (f32[2,2,512]{2,1,0:T(2,128)S(1)}, f32[2,2,512]{2,1,0:T(2,128)}, u32[]{:S(2)}) copy-start(f32[2,2,512]{2,1,0:T(2,128)} %param.7) | copy-start | bytes 24580
Sparse Core Ops, SparseCore 0:
  23.9 44.0 reduce-scatter.7
  70.5 37.2 reduce-scatter.5
  113.2 261.4 all-reduce.2
where the time goes:
time: 384 us; the launch traced here: 383 us
  waiting for transfers between devices  341 us (89%)
  between operations  13.9 us (4%)
  other arithmetic  11 us (3%)
  matrix products  9.19 us (2%)
  local copies, waits for them, and re-layouts  7.23 us (2%)
    unnamed x4, waiting for transfers between devices  262 us
    reduce_scatter x1, waiting for transfers between devices, local(): lax.psum_scatter(jnp.dot(ancestor_inverse, joined, preferred_element_type...  41.3 us
    reduce_scatter x1, waiting for transfers between devices, local(): lax.psum_scatter(contribution.astype(jnp.bfloat16), 'pcol', scatter_dimen...  38.2 us
  transfers between devices with their start and end apart: 3, of which 3 were waited for; matrix products, arithmetic and copies ran while one was open for 2% of the time, Pallas kernels for 0%

commit v1 on v0

v1 whole, which is shorter than its diff:
```python
import jax
import jax.numpy as jnp
import numpy as np
from jax import lax
from jax.experimental import pallas as pl
from jax.experimental.pallas import tpu as pltpu
from jax.sharding import Mesh
from jax.sharding import PartitionSpec as P

BLOCK = 128
VMEM = pltpu.VMEM
BF16 = jnp.bfloat16
F32 = jnp.float32


def params(**kw):
    return pltpu.CompilerParams(vmem_limit_bytes=40 * 1024 * 1024, **kw)


def whole():
    return pl.BlockSpec(memory_space=VMEM)


def scalars():
    return pl.BlockSpec(memory_space=pltpu.SMEM)


def product(place, ancestor, panel, pattern, kind):
    height, breadth = ancestor.shape
    wide = panel.shape[2]
    step = 512
    steps = breadth // step

    def kernel(place_ref, a_ref, l_ref, p_ref, o_ref, acc):
        k = pl.program_id(0)
        row = p_ref[pl.ds(place_ref[0], 1), :]
        first = place_ref[1] + k * (step // BLOCK)
        parts = []
        for b in range(step // BLOCK):
            hit = jnp.max(jnp.where(row == first + b, 1.0, 0.0).astype(F32), axis=1, keepdims=True)
            parts.append(l_ref[0, b * BLOCK : (b + 1) * BLOCK, :] * hit.astype(BF16))
        masked = jnp.concatenate(parts, axis=0)
        term = jnp.dot(a_ref[...], masked, preferred_element_type=F32)

        @pl.when(k == 0)
        def _():
            acc[...] = term

        @pl.when(jnp.logical_and(k > 0, k < steps - 1))
        def _():
            acc[...] += term

        @pl.when(k == steps - 1)
        def _():
            o_ref[...] = (acc[...] + term).astype(kind)

    return pl.pallas_call(
        kernel,
        grid_spec=pltpu.PrefetchScalarGridSpec(
            num_scalar_prefetch=1,
            grid=(steps,),
            in_specs=[
                pl.BlockSpec((height, step), lambda k, at: (0, k)),
                pl.BlockSpec((1, step, wide), lambda k, at: (at[0], k, 0)),
                pl.BlockSpec(pattern.shape, lambda k, at: (0, 0)),
            ],
            out_specs=pl.BlockSpec((height, wide), lambda k, at: (0, 0)),
            scratch_shapes=[pltpu.VMEM((height, wide), F32)],
        ),
        out_shape=jax.ShapeDtypeStruct((height, wide), kind),
        compiler_params=params(),
        cost_estimate=pl.CostEstimate(
            flops=2 * height * breadth * wide,
            bytes_accessed=2 * (height * breadth + breadth * wide + height * wide),
            transcendentals=0,
        ),
        name="product",
    )(place, ancestor, panel, pattern)


def join(place, own, arrived, lines):
    height, wide = own.shape
    part = height // lines

    def kernel(place_ref, own_ref, in_ref, keep_ref, *sent):
        here = place_ref[0]
        for m in range(lines):
            rows = pl.ds(pl.multiple_of((here ^ m) * part, 16), part)
            total = own_ref[rows, :] + in_ref[rows, :].astype(F32)
            if m == 0:
                keep_ref[...] = total
            else:
                sent[m - 1][...] = total.astype(BF16)

    piece = jax.ShapeDtypeStruct((part, wide), BF16)
    return pl.pallas_call(
        kernel,
        in_specs=[scalars(), whole(), whole()],
        out_specs=[whole()] * lines,
        out_shape=[jax.ShapeDtypeStruct((part, wide), F32)] + [piece] * (lines - 1),
        compiler_params=params(),
        name="join",
    )(place, own, arrived)


def contract(place, pattern, mine, keep, arrived):
    part, wide = keep.shape
    half = part // 2

    def kernel(place_ref, p_ref, m_ref, keep_ref, *rest):
        ins, (own_ref, send_ref, g_ref, off) = rest[: len(arrived)], rest[len(arrived) :]
        total = keep_ref[...]
        for r in ins:
            total = total + r[...].astype(F32)
        row = p_ref[pl.ds(place_ref[0], 1), :]
        ids = (place_ref[1] + lax.broadcasted_iota(jnp.int32, (part, 1), 0)) >> 7
        hit = jnp.max(jnp.where(ids == row, 1.0, 0.0).astype(F32), axis=1, keepdims=True)
        off[...] = -(total * hit)
        core = place_ref[2]
        own_ref[...] = off[pl.ds(pl.multiple_of(core * half, 16), half), :].astype(BF16)
        send_ref[...] = off[pl.ds(pl.multiple_of((1 - core) * half, 16), half), :].astype(BF16)
        masked = m_ref[...] * hit.astype(BF16)
        g = lax.dot_general(masked, total.astype(BF16), (((0,), (0,)), ((), ())), preferred_element_type=F32)
        g_ref[...] = g.astype(BF16)

    piece = jax.ShapeDtypeStruct((half, wide), BF16)
    return pl.pallas_call(
        kernel,
        in_specs=[scalars()] + [whole()] * (3 + len(arrived)),
        out_specs=[whole()] * 3,
        out_shape=[piece, piece, jax.ShapeDtypeStruct((wide, wide), BF16)],
        scratch_shapes=[pltpu.VMEM((part, wide), F32)],
        compiler_params=params(),
        name="contract",
    )(place, pattern, mine, keep, *arrived)


def solution(mesh):
    cut = Mesh(mesh.devices.reshape(2, 4, 4, 4, 2), ("zh", "x", "y", "zl", "c"))
    every = ("zh", "x", "y", "zl", "c")
    xor4 = {m: [(i, i ^ m) for i in range(4)] for m in (1, 2, 3)}
    swap = [(0, 1), (1, 0)]
    fetch = []
    for zh in range(2):
        for x in range(4):
            for y in range(4):
                for p in range(8):
                    source = ((zh * 4 + x) * 4 + y) * 8 + p
                    fetch.append((source, (p * 4 + y) * 8 + (2 * zh + (x >> 1)) * 2 + (x & 1)))

    def local(ancestor, panel, pattern, diag):
        height, breadth = ancestor.shape
        wide = panel.shape[2]
        zh, x, y, zl, c = (lax.axis_index(a) for a in every)
        part = height // 4
        columns = (zl * 2 + c) * (breadth // BLOCK)
        first = ((zh * 4 + x) * 4 + y) * height + zl * part

        fetched = lax.dynamic_slice(
            panel, (x & 1, y * height + (2 * zh + (x >> 1)) * part, 0), (1, part, wide)
        )[0]
        mine = lax.ppermute(fetched, every, fetch)

        other = product(jnp.stack([1 - c, columns]), ancestor, panel, pattern, BF16)
        swapped = lax.ppermute(other, "c", swap)
        own = product(jnp.stack([c, columns]), ancestor, panel, pattern, F32)
        keep, *sent = join(jnp.stack([zl]), own, swapped, 4)
        arrived = [lax.ppermute(sent[m - 1], "zl", xor4[m]) for m in (3, 2, 1)]
        off_own, off_send, g = contract(jnp.stack([c, first, c]), pattern, mine, keep, arrived)
        off_other = lax.ppermute(off_send, "c", swap)
        off = jnp.where(c == 0, jnp.stack([off_own, off_other]), jnp.stack([off_other, off_own]))
        pieces = lax.all_to_all(g.reshape(256, 2, wide), every, 0, 0, tiled=True)
        total = jnp.sum(pieces.reshape(128, 2, 2, wide).astype(F32), axis=0)
        return off, diag + total

    rows = ("zh", "x", "y")
    cols = ("zl", "c")
    return jax.shard_map(
        local,
        mesh=cut,
        in_specs=(P(rows, cols), P(None, cols, None), P(), P(None, every, None)),
        out_specs=(P(None, every, None), P(None, every, None)),
        check_vma=False,
    )
```

time: 384 us -> 81.1 us (0.21)
  waiting for transfers between devices: 341 us -> 30.1 us
  starting transfers between devices: 0.12 us -> 26.1 us
  between operations: 13.9 us -> 0.72 us
  Pallas kernels: 0 us -> 11.7 us
  matrix products: 9.19 us -> 0 us
  other arithmetic: 11 us -> 1.99 us
    unnamed x4 -> x0, waiting for transfers between devices: 262 us -> none
    reduce_scatter x2 -> x0, waiting for transfers between devices: 79.5 us -> none  [the longest x1 41.3 us: local(): lax.psum_scatter(jnp.dot(ancestor_inverse, joined, preferred_element_type...]
    all_to_all x0 -> x1, waiting for transfers between devices: none -> 16.2 us  [local(): pieces = lax.all_to_all(g.reshape(256, 2, wide), every, 0, 0, tiled=True)]
    ppermute x0 -> x6, starting transfers between devices: none -> 15.4 us  [the longest x3 8 us: local(): arrived = [lax.ppermute(sent[m - 1], 'zl', xor4[m]) for m in (3, 2, 1)]]
    ppermute x0 -> x6, waiting for transfers between devices: none -> 13.9 us  [the longest x3 13 us: local(): arrived = [lax.ppermute(sent[m - 1], 'zl', xor4[m]) for m in (3, 2, 1)]]
    pallas_call x0 -> x4, Pallas kernels: none -> 11.7 us  [the longest x2 9.52 us: product(): pl.pallas_call(kernel, grid_spec=pltpu.PrefetchScalarGridSpec(num_scalar_...]
    all_to_all x0 -> x1, starting transfers between devices: none -> 10.7 us  [local(): pieces = lax.all_to_all(g.reshape(256, 2, wide), every, 0, 0, tiled=True)]
    dot_general x2 -> x0, matrix products: 9.19 us -> none  [the longest x1 5.83 us: local(): jnp.dot(ancestor_inverse, joined, preferred_element_type=jnp.float32)]
  transfers between devices with their start and end apart: 3 -> 7, of which waited for: 3 -> 4; matrix products, arithmetic and copies ran while one was open for 2% -> 3% of each run, Pallas kernels for 0% -> 7%
where the time goes in v1:
time: 81.1 us; the launch traced here: 80.8 us
  waiting for transfers between devices  30.1 us (37%)
  starting transfers between devices  26.1 us (32%)
  Pallas kernels  11.7 us (14%)
  local copies, waits for them, and re-layouts  10.2 us (13%)
  other arithmetic  1.99 us (2%)
    all_to_all x1, waiting for transfers between devices, local(): pieces = lax.all_to_all(g.reshape(256, 2, wide), every, 0, 0, tiled=True)  16.2 us
    ppermute x3, waiting for transfers between devices, local(): arrived = [lax.ppermute(sent[m - 1], 'zl', xor4[m]) for m in (3, 2, 1)]  13 us
    all_to_all x1, starting transfers between devices, local(): pieces = lax.all_to_all(g.reshape(256, 2, wide), every, 0, 0, tiled=True)  10.7 us
    pallas_call x2, Pallas kernels, product(): pl.pallas_call(kernel, grid_spec=pltpu.PrefetchScalarGridSpec(num_scalar_...  9.52 us
    ppermute x3, starting transfers between devices, local(): arrived = [lax.ppermute(sent[m - 1], 'zl', xor4[m]) for m in (3, 2, 1)]  8 us
    unnamed x14, local copies, waits for them, and re-layouts  7.59 us
    ppermute x1, starting transfers between devices, local(): swapped = lax.ppermute(other, 'c', swap)  3.24 us
    ppermute x1, starting transfers between devices, local(): off_other = lax.ppermute(off_send, 'c', swap)  2.23 us
  transfers between devices with their start and end apart: 7, of which 4 were waited for; matrix products, arithmetic and copies ran while one was open for 3% of the time, Pallas kernels for 7%

profile of v1, /device:TPU:1, one launch (start us, length us, event | category | flops | bytes accessed | tf_op | source)
XLA Modules:
  0.0 80.8 jit_solution(5401993633685470930)
XLA Ops:
  0.7 2.5 %copy-done = bf16[2,2560,512]{2,1,0:T(8,128)(2,1)S(1)} copy-done((bf16[2,2560,512]{2,1,0:T(8,128)(2,1)S(1)}, bf16[2,2560,512]{2,1,0:T(8,128)(2,1)}, u32[]{:S(2)}) %copy-start) | copy-done | bytes 5242904
  3.2 1.9 %copy-done.2 = bf16[640,2560]{1,0:T(8,128)(2,1)S(1)} copy-done((bf16[640,2560]{1,0:T(8,128)(2,1)S(1)}, bf16[640,2560]{1,0:T(8,128)(2,1)}, u32[]{:S(2)}) %copy-start.2) | copy-done | bytes 3276824
  5.1 0.7 copy-done.4
  5.8 5.2 %product.3 = bf16[640,512]{1,0:T(8,128)(2,1)} custom-call(s32[2]{0:T(128)S(1)} %pad_add_fusion.2.place_ref, bf16[640,2560]{1,0:T(8,128)(2,1)S(1)} %copy-done.2, bf16[2,2560,512]{2,1,0:T(8,128)(2,1)S(1)} %copy-done, s32[2,80]{1,0:T(2,128)S(1)} %copy-done.4), custom_call_target="tpu_custom_call" | custom-call | flops 1677721600 | bytes 6553600 | tf_op jit(solution)/shard_map/product/pallas_call | solution.py:57
  11.0 3.2 %collective-permute-start.1 = (bf16[640,512]{1,0:T(8,128)(2,1)}, bf16[640,512]{1,0:T(8,128)(2,1)}, u32[]{:S(2)}, u32[]{:S(2)}) collective-permute-start(bf16[640,512]{1,0:T(8,128)(2,1)} %product.3), channel_id=1, source_target_pairs={{0,1},{1,0},{2,3},{3,2},{4,5},{5,4},{6,7},{7,6},{8,9},{9,8},{10,11... | collective-permute-start | bytes 1966088 | tf_op jit(solution)/shard_map/ppermute | solution.py:165
  14.2 1.6 %dynamic-slice_bitcast_fusion = bf16[160,512]{1,0:T(8,128)(2,1)} fusion(bf16[2,2560,512]{2,1,0:T(8,128)(2,1)} %l_ref.3, s32[]{:T(128)S(6)} %select_n.15, s32[]{:T(128)S(6)} %select_n.16), kind=kLoop, calls=%fused_computation.2 | loop fusion | bytes 327688 | tf_op jit(solution)/shard_map/squeeze | solution.py:159
  15.8 1.9 %collective-permute-start = (bf16[160,512]{1,0:T(8,128)(2,1)}, bf16[160,512]{1,0:T(8,128)(2,1)S(1)}, u32[]{:S(2)}, u32[]{:S(2)}) collective-permute-start(bf16[160,512]{1,0:T(8,128)(2,1)} %dynamic-slice_bitcast_fusion), channel_id=1, source_target_pairs={{0,0},{1,32},{2,64},{3,96},{4,128},{5,160},{6,192},{7,224},{8,8},{... | collective-permute-start | bytes 491528 | tf_op jit(solution)/shard_map/ppermute | solution.py:162
  17.7 0.1 pad_add_fusion.1.place_ref
  17.8 2.5 %copy-done.1 = bf16[2,2560,512]{2,1,0:T(8,128)(2,1)S(1)} copy-done((bf16[2,2560,512]{2,1,0:T(8,128)(2,1)S(1)}, bf16[2,2560,512]{2,1,0:T(8,128)(2,1)}, u32[]{:S(2)}) %copy-start.1) | copy-done | bytes 5242904
  20.3 4.3 %product.2.own_ref = f32[640,512]{1,0:T(8,128)S(1)} custom-call(s32[2]{0:T(128)S(1)} %pad_add_fusion.1.place_ref, bf16[640,2560]{1,0:T(8,128)(2,1)S(1)} %copy-done.3, bf16[2,2560,512]{2,1,0:T(8,128)(2,1)S(1)} %copy-done.1, s32[2,80]{1,0:T(2,128)S(1)} %copy-done.5), custom_call_target="tpu_custom_call" | custom-call | flops 1677721600 | bytes 6553600 | tf_op jit(solution)/shard_map/product/pallas_call | solution.py:57
  24.7 1.2 %join.1 = (f32[160,512]{1,0:T(8,128)S(1)}, bf16[160,512]{1,0:T(8,128)(2,1)S(1)}, bf16[160,512]{1,0:T(8,128)(2,1)S(1)}, bf16[160,512]{1,0:T(8,128)(2,1)S(1)}) custom-call(s32[1]{0:T(128)} %bitcast.3.place_ref, f32[640,512]{1,0:T(8,128)S(1)} %product.2.own_ref, bf16[640,512]{1,0:T(8,128)(2,1)} %collective-permute-done.1.in_ref), custom_call_target="tpu_custom_call" | custom-call | tf_op jit(solution)/shard_map/join/pallas_call | solution.py:96
  25.9 7.6 %collective-permute-start.2 = (bf16[160,512]{1,0:T(8,128)(2,1)S(1)}, bf16[160,512]{1,0:T(8,128)(2,1)S(1)}, u32[]{:S(2)}, u32[]{:S(2)}) collective-permute-start(bf16[160,512]{1,0:T(8,128)(2,1)S(1)} %get-tuple-element.10), channel_id=1, source_target_pairs={{0,6},{2,4},{4,2},{6,0},{1,7},{3,5},{5,3},{7,1},{8,14},{10,12},{12... | collective-permute-start | bytes 491528 | tf_op jit(solution)/shard_map/ppermute | solution.py:168
  33.5 0.4 collective-permute-start.4
  34.0 3.5 %collective-permute-done.2.rest_0_ = bf16[160,512]{1,0:T(8,128)(2,1)S(1)} collective-permute-done((bf16[160,512]{1,0:T(8,128)(2,1)S(1)}, bf16[160,512]{1,0:T(8,128)(2,1)S(1)}, u32[]{:S(2)}, u32[]{:S(2)}) %collective-permute-start.2) | collective-permute-done | bytes 163872 | tf_op jit(solution)/shard_map/ppermute | solution.py:168
  37.5 9.4 %collective-permute-done.3.rest_1_ = bf16[160,512]{1,0:T(8,128)(2,1)S(1)} collective-permute-done((bf16[160,512]{1,0:T(8,128)(2,1)S(1)}, bf16[160,512]{1,0:T(8,128)(2,1)S(1)}, u32[]{:S(2)}, u32[]{:S(2)}) %collective-permute-start.3) | collective-permute-done | bytes 163872 | tf_op jit(solution)/shard_map/ppermute | solution.py:168
  46.9 1.0 %contract.1 = (bf16[80,512]{1,0:T(8,128)(2,1)S(1)}, bf16[80,512]{1,0:T(8,128)(2,1)S(1)}, bf16[512,512]{1,0:T(8,128)(2,1)S(1)}) custom-call(s32[3]{0:T(128)S(1)} %pad_add_fusion.place_ref, s32[2,80]{1,0:T(2,128)S(1)} %copy-done.5, bf16[160,512]{1,0:T(8,128)(2,1)S(1)} %collective-permute-done.m_ref, f32[160,512]{1,0:T(8,128)S(1)} %get-tuple-element.9.keep_ref, ...), custom_call_target="tpu_custom_call" | custom-call | tf_op jit(solution)/shard_map/contract/pallas_call | solution.py:127
  47.9 1.0 %reshape.10 = bf16[256,2,512]{2,1,0:T(2,128)(2,1)} reshape(bf16[512,512]{1,0:T(8,128)(2,1)S(1)} %get-tuple-element.15) | data formatting | bytes 1048576 | tf_op jit(solution)/shard_map/reshape | solution.py:172
  48.9 10.7 %all-to-all-start = ((bf16[256,2,512]{2,1,0:T(2,128)(2,1)}), bf16[256,2,512]{2,1,0:T(2,128)(2,1)S(1)}, u32[]{:S(2)}, u32[]{:S(2)}) async-start(bf16[256,2,512]{2,1,0:T(2,128)(2,1)} %reshape.10), calls=%async_computation | async-start | bytes 1048576 | tf_op jit(solution)/shard_map/all_to_all | solution.py:172
  59.6 2.2 %collective-permute-start.5 = (bf16[80,512]{1,0:T(8,128)(2,1)S(1)}, bf16[80,512]{1,0:T(8,128)(2,1)S(1)}, u32[]{:S(2)}, u32[]{:S(2)}) collective-permute-start(bf16[80,512]{1,0:T(8,128)(2,1)S(1)} %get-tuple-element.14), channel_id=1, source_target_pairs={{0,1},{1,0},{2,3},{3,2},{4,5},{5,4},{6,7},{7,6},{8,9},{9,8},{10,11... | collective-permute-start | bytes 245768 | tf_op jit(solution)/shard_map/ppermute | solution.py:170
  61.8 0.9 %collective-permute-done.5 = bf16[80,512]{1,0:T(8,128)(2,1)S(1)} collective-permute-done((bf16[80,512]{1,0:T(8,128)(2,1)S(1)}, bf16[80,512]{1,0:T(8,128)(2,1)S(1)}, u32[]{:S(2)}, u32[]{:S(2)}) %collective-permute-start.5) | collective-permute-done | bytes 81952 | tf_op jit(solution)/shard_map/ppermute | solution.py:170
  62.8 0.7 maximum_select_fusion
  63.5 16.2 %all-to-all-done = bf16[256,2,512]{2,1,0:T(2,128)(2,1)S(1)} async-done(((bf16[256,2,512]{2,1,0:T(2,128)(2,1)}), bf16[256,2,512]{2,1,0:T(2,128)(2,1)S(1)}, u32[]{:S(2)}, u32[]{:S(2)}) %all-to-all-start) | async-done | bytes 524320 | tf_op jit(solution)/shard_map/all_to_all | solution.py:172
  79.7 0.5 convert_reduce_fusion
  80.2 0.6 add.35
  (16 shorter events, 0.2 us)
Async XLA Ops:
  0.6 17.2 %copy-start.5 = (s32[2,80]{1,0:T(2,128)S(1)}, s32[2,80]{1,0:T(2,128)}, u32[]{:S(2)}) copy-start(s32[2,80]{1,0:T(2,128)} %p_ref.5) | copy-start | bytes 1924
  0.7 2.5 %copy-start = (bf16[2,2560,512]{2,1,0:T(8,128)(2,1)S(1)}, bf16[2,2560,512]{2,1,0:T(8,128)(2,1)}, u32[]{:S(2)}) copy-start(bf16[2,2560,512]{2,1,0:T(8,128)(2,1)} %l_ref.3) | copy-start | bytes 15728644
  3.2 1.9 %copy-start.2 = (bf16[640,2560]{1,0:T(8,128)(2,1)S(1)}, bf16[640,2560]{1,0:T(8,128)(2,1)}, u32[]{:S(2)}) copy-start(bf16[640,2560]{1,0:T(8,128)(2,1)} %a_ref.3) | copy-start | bytes 9830404
  5.1 0.7 copy-start.4
  5.8 12.0 %copy-start.3 = (bf16[640,2560]{1,0:T(8,128)(2,1)S(1)}, bf16[640,2560]{1,0:T(8,128)(2,1)}, u32[]{:S(2)}) copy-start(bf16[640,2560]{1,0:T(8,128)(2,1)} %a_ref.3) | copy-start | bytes 9830404
  11.0 13.7 %collective-permute-start.1 = (bf16[640,512]{1,0:T(8,128)(2,1)}, bf16[640,512]{1,0:T(8,128)(2,1)}, u32[]{:S(2)}, u32[]{:S(2)}) collective-permute-start(bf16[640,512]{1,0:T(8,128)(2,1)} %product.3), channel_id=1, source_target_pairs={{0,1},{1,0},{2,3},{3,2},{4,5},{5,4},{6,7},{7,6},{8,9},{9,8},{10,11... | collective-permute-start | bytes 1966088 | tf_op jit(solution)/shard_map/ppermute | solution.py:165
  15.8 18.1 %collective-permute-start = (bf16[160,512]{1,0:T(8,128)(2,1)}, bf16[160,512]{1,0:T(8,128)(2,1)S(1)}, u32[]{:S(2)}, u32[]{:S(2)}) collective-permute-start(bf16[160,512]{1,0:T(8,128)(2,1)} %dynamic-slice_bitcast_fusion), channel_id=1, source_target_pairs={{0,0},{1,32},{2,64},{3,96},{4,128},{5,160},{6,192},{7,224},{8,8},{... | collective-permute-start | bytes 491528 | tf_op jit(solution)/shard_map/ppermute | solution.py:162
  17.8 2.5 %copy-start.1 = (bf16[2,2560,512]{2,1,0:T(8,128)(2,1)S(1)}, bf16[2,2560,512]{2,1,0:T(8,128)(2,1)}, u32[]{:S(2)}) copy-start(bf16[2,2560,512]{2,1,0:T(8,128)(2,1)} %l_ref.3) | copy-start | bytes 15728644
  24.7 55.5 %copy-start.6 = (f32[2,2,512]{2,1,0:T(2,128)S(1)}, f32[2,2,512]{2,1,0:T(2,128)}, u32[]{:S(2)}) copy-start(f32[2,2,512]{2,1,0:T(2,128)} %param.7) | copy-start | bytes 24580
  25.9 11.6 %collective-permute-start.2 = (bf16[160,512]{1,0:T(8,128)(2,1)S(1)}, bf16[160,512]{1,0:T(8,128)(2,1)S(1)}, u32[]{:S(2)}, u32[]{:S(2)}) collective-permute-start(bf16[160,512]{1,0:T(8,128)(2,1)S(1)} %get-tuple-element.10), channel_id=1, source_target_pairs={{0,6},{2,4},{4,2},{6,0},{1,7},{3,5},{5,3},{7,1},{8,14},{10,12},{12... | collective-permute-start | bytes 491528 | tf_op jit(solution)/shard_map/ppermute | solution.py:168
  33.5 13.4 %collective-permute-start.3 = (bf16[160,512]{1,0:T(8,128)(2,1)S(1)}, bf16[160,512]{1,0:T(8,128)(2,1)S(1)}, u32[]{:S(2)}, u32[]{:S(2)}) collective-permute-start(bf16[160,512]{1,0:T(8,128)(2,1)S(1)} %get-tuple-element.11), channel_id=1, source_target_pairs={{0,4},{2,6},{4,0},{6,2},{1,5},{3,7},{5,1},{7,3},{8,12},{10,14},{12... | collective-permute-start | bytes 491528 | tf_op jit(solution)/shard_map/ppermute | solution.py:168
  33.5 13.4 %collective-permute-start.4 = (bf16[160,512]{1,0:T(8,128)(2,1)S(1)}, bf16[160,512]{1,0:T(8,128)(2,1)S(1)}, u32[]{:S(2)}, u32[]{:S(2)}) collective-permute-start(bf16[160,512]{1,0:T(8,128)(2,1)S(1)} %get-tuple-element.12), channel_id=1, source_target_pairs={{0,2},{2,0},{4,6},{6,4},{1,3},{3,1},{5,7},{7,5},{8,10},{10,8},{12,... | collective-permute-start | bytes 491528 | tf_op jit(solution)/shard_map/ppermute | solution.py:168
  48.9 30.8 %all-to-all-start = ((bf16[256,2,512]{2,1,0:T(2,128)(2,1)}), bf16[256,2,512]{2,1,0:T(2,128)(2,1)S(1)}, u32[]{:S(2)}, u32[]{:S(2)}) async-start(bf16[256,2,512]{2,1,0:T(2,128)(2,1)} %reshape.10), calls=%async_computation | async-start | bytes 1048576 | tf_op jit(solution)/shard_map/all_to_all | solution.py:172
  59.6 3.2 %collective-permute-start.5 = (bf16[80,512]{1,0:T(8,128)(2,1)S(1)}, bf16[80,512]{1,0:T(8,128)(2,1)S(1)}, u32[]{:S(2)}, u32[]{:S(2)}) collective-permute-start(bf16[80,512]{1,0:T(8,128)(2,1)S(1)} %get-tuple-element.14), channel_id=1, source_target_pairs={{0,1},{1,0},{2,3},{3,2},{4,5},{5,4},{6,7},{7,6},{8,9},{9,8},{10,11... | collective-permute-start | bytes 245768 | tf_op jit(solution)/shard_map/ppermute | solution.py:170

commit v2 on v1

v2 whole, which is shorter than its diff:
```python
import jax
import jax.numpy as jnp
import numpy as np
from jax import lax
from jax.experimental import pallas as pl
from jax.experimental.pallas import tpu as pltpu
from jax.sharding import Mesh
from jax.sharding import PartitionSpec as P

BLOCK = 128
VMEM = pltpu.VMEM
BF16 = jnp.bfloat16
F32 = jnp.float32


def params(mib=40):
    return pltpu.CompilerParams(vmem_limit_bytes=mib * 1024 * 1024)


def whole():
    return pl.BlockSpec(memory_space=VMEM)


def scalars():
    return pl.BlockSpec(memory_space=pltpu.SMEM)


def place_of(me):
    return me >> 7, (me >> 5) & 3, (me >> 3) & 3, (me >> 1) & 3, me & 1


def masked(rows, pattern_row, first):
    parts = []
    for b in range(rows.shape[0] // BLOCK):
        hit = jnp.max(jnp.where(pattern_row == first + b, 1.0, 0.0).astype(F32), axis=1, keepdims=True)
        parts.append(rows[b * BLOCK : (b + 1) * BLOCK, :] * hit.astype(BF16))
    return jnp.concatenate(parts, axis=0)


def hbm():
    return pl.BlockSpec(memory_space=pltpu.HBM)


STEP = 512
LIMIT = 50


def cost(height, breadth, wide):
    return pl.CostEstimate(
        flops=2 * height * breadth * wide,
        bytes_accessed=2 * (height * breadth + breadth * wide + height * wide),
        transcendentals=0,
    )


def products(me, ancestor, panel, pattern):
    height, breadth = ancestor.shape
    wide = panel.shape[2]
    steps = breadth // STEP
    part = height // 4

    def kernel(me_ref, a_hbm, l_hbm, p_hbm, o_ref, k_ref, f_ref, p_ref, a_buf, l_buf, acc, a_sem, l_sem, f_sem, p_sem):
        zh, x, y, zl, c = place_of(me_ref[0])
        listed = pltpu.make_async_copy(p_hbm, p_ref, p_sem)
        listed.start()
        order = (1 - c, c)
        a_copies, l_copies = [], []
        for k in range(steps):
            cols = pl.ds(k * STEP, STEP)
            a_copies.append(pltpu.make_async_copy(a_hbm.at[:, cols], a_buf.at[k], a_sem.at[k]))
            l_copies.append(
                [
                    pltpu.make_async_copy(l_hbm.at[order[i], cols, :], l_buf.at[i, k], l_sem.at[i, k])
                    for i in range(2)
                ]
            )
            a_copies[k].start()
            l_copies[k][0].start()
            l_copies[k][1].start()
        start = pl.multiple_of(y * height + (2 * zh + (x >> 1)) * part, 16)
        fetch = pltpu.make_async_copy(l_hbm.at[x & 1, pl.ds(start, part), :], f_ref, f_sem)
        fetch.start()
        listed.wait()
        first = (zl * 2 + c) * (breadth // BLOCK)
        for k in range(steps):
            a_copies[k].wait()
            for i in range(2):
                l_copies[k][i].wait()
                row = p_ref[pl.ds(order[i], 1), :]
                rows = masked(l_buf[i, k], row, first + k * (STEP // BLOCK))
                term = jnp.dot(a_buf[k], rows, preferred_element_type=F32)
                total = acc if i == 0 else k_ref
                if k == 0:
                    total[...] = term
                elif k == steps - 1 and i == 0:
                    o_ref[...] = (total[...] + term).astype(BF16)
                else:
                    total[...] += term
        fetch.wait()

    return pl.pallas_call(
        kernel,
        in_specs=[scalars(), hbm(), hbm(), hbm()],
        out_specs=[whole(), whole(), whole()],
        out_shape=[
            jax.ShapeDtypeStruct((height, wide), BF16),
            jax.ShapeDtypeStruct((height, wide), F32),
            jax.ShapeDtypeStruct((part, wide), BF16),
        ],
        scratch_shapes=[
            pltpu.VMEM(pattern.shape, pattern.dtype),
            pltpu.VMEM((steps, height, STEP), BF16),
            pltpu.VMEM((2, steps, STEP, wide), BF16),
            pltpu.VMEM((height, wide), F32),
            pltpu.SemaphoreType.DMA((steps,)),
            pltpu.SemaphoreType.DMA((2, steps)),
            pltpu.SemaphoreType.DMA,
            pltpu.SemaphoreType.DMA,
        ],
        compiler_params=params(LIMIT),
        cost_estimate=cost(height, breadth, 2 * wide),
        name="products",
    )(me, ancestor, panel, pattern)


def join(me, own, arrived, lines):
    height, wide = own.shape
    part = height // lines

    def kernel(me_ref, own_ref, in_ref, keep_ref, *sent):
        here = place_of(me_ref[0])[3]
        for m in range(lines):
            rows = pl.ds(pl.multiple_of((here ^ m) * part, 16), part)
            total = own_ref[rows, :] + in_ref[rows, :].astype(F32)
            if m == 0:
                keep_ref[...] = total
            else:
                sent[m - 1][...] = total.astype(BF16)

    piece = jax.ShapeDtypeStruct((part, wide), BF16)
    return pl.pallas_call(
        kernel,
        in_specs=[scalars(), whole(), whole()],
        out_specs=[whole()] * lines,
        out_shape=[jax.ShapeDtypeStruct((part, wide), F32)] + [piece] * (lines - 1),
        compiler_params=params(),
        name="join",
    )(me, own, arrived)


def contract(me, height, pattern, mine, keep, arrived):
    part, wide = keep.shape
    half = part // 2

    def kernel(me_ref, p_ref, m_ref, keep_ref, *rest):
        zh, x, y, zl, core = place_of(me_ref[0])
        first = ((zh * 4 + x) * 4 + y) * height + zl * part
        ins, (own_ref, send_ref, g_ref, off) = rest[: len(arrived)], rest[len(arrived) :]
        total = keep_ref[...]
        for r in ins:
            total = total + r[...].astype(F32)
        row = p_ref[pl.ds(core, 1), :]
        ids = (first + lax.broadcasted_iota(jnp.int32, (part, 1), 0)) >> 7
        hit = jnp.max(jnp.where(ids == row, 1.0, 0.0).astype(F32), axis=1, keepdims=True)
        off[...] = -(total * hit)
        own_ref[...] = off[pl.ds(pl.multiple_of(core * half, 16), half), :].astype(BF16)
        send_ref[...] = off[pl.ds(pl.multiple_of((1 - core) * half, 16), half), :].astype(BF16)
        chosen = m_ref[...] * hit.astype(BF16)
        g = lax.dot_general(chosen, total.astype(BF16), (((0,), (0,)), ((), ())), preferred_element_type=F32)
        g = g.astype(BF16)
        groups, both = g_ref.shape[0], g_ref.shape[1] // 2
        for i in range(groups):
            for h in range(2):
                start = h * (wide // 2) + i * both
                g_ref[i, h * both : (h + 1) * both, :] = g[start : start + both, :]

    piece = jax.ShapeDtypeStruct((half, wide), BF16)
    return pl.pallas_call(
        kernel,
        in_specs=[scalars()] + [whole()] * (3 + len(arrived)),
        out_specs=[whole()] * 3,
        out_shape=[piece, piece, jax.ShapeDtypeStruct((16, wide // 16, wide), BF16)],
        scratch_shapes=[pltpu.VMEM((part, wide), F32)],
        compiler_params=params(),
        name="contract",
    )(me, pattern, mine, keep, *arrived)


def gather(pieces):
    count, tall, wide = pieces.shape

    def kernel(in_ref, o_ref):
        total = in_ref[0].astype(F32)
        for i in range(1, count):
            total = total + in_ref[i].astype(F32)
        for j in range(tall // 2):
            o_ref[j] = total[2 * j : 2 * j + 2, :].astype(o_ref.dtype)

    return pl.pallas_call(
        kernel,
        in_specs=[whole()],
        out_specs=whole(),
        out_shape=jax.ShapeDtypeStruct((tall // 2, 2, wide), F32),
        compiler_params=params(),
        name="gather",
    )(pieces)


def finish(pieces, diag):
    def kernel(in_ref, d_ref, o_ref):
        for s in range(2):
            total = in_ref[s]
            for i in range(s + 2, in_ref.shape[0], 2):
                total = total + in_ref[i]
            o_ref[s] = d_ref[s] + total

    return pl.pallas_call(
        kernel,
        in_specs=[whole(), whole()],
        out_specs=whole(),
        out_shape=jax.ShapeDtypeStruct(diag.shape, F32),
        compiler_params=params(),
        name="finish",
    )(pieces, diag)


def solution(mesh):
    cut = Mesh(mesh.devices.reshape(2, 4, 4, 4, 2), ("zh", "x", "y", "zl", "c"))
    every = ("zh", "x", "y", "zl", "c")
    xor4 = {m: [(i, i ^ m) for i in range(4)] for m in (1, 2, 3)}
    swap = [(0, 1), (1, 0)]
    fetch = []
    for zh in range(2):
        for x in range(4):
            for y in range(4):
                for p in range(8):
                    source = ((zh * 4 + x) * 4 + y) * 8 + p
                    fetch.append((source, (p * 4 + y) * 8 + (2 * zh + (x >> 1)) * 2 + (x & 1)))

    def local(ancestor, panel, pattern, diag):
        me = jnp.reshape(lax.axis_index(every), (1,))
        core = lax.axis_index("c")
        other, own, fetched = products(me, ancestor, panel, pattern)
        swapped = lax.ppermute(other, "c", swap)
        mine = lax.ppermute(fetched, every, fetch)
        keep, *sent = join(me, own, swapped, 4)
        arrived = [lax.ppermute(sent[m - 1], "zl", xor4[m]) for m in (3, 2, 1)]
        off_own, off_send, g = contract(me, ancestor.shape[0], pattern, mine, keep, arrived)
        pieces = lax.all_to_all(g, ("x", "y"), 0, 0, tiled=True)
        off_other = lax.ppermute(off_send, "c", swap)
        off = jnp.where(core == 0, jnp.stack([off_own, off_other]), jnp.stack([off_other, off_own]))
        pieces = lax.all_to_all(gather(pieces), ("zh", "zl", "c"), 0, 0, tiled=True)
        return off, finish(pieces, diag)

    rows = ("zh", "x", "y")
    cols = ("zl", "c")
    return jax.shard_map(
        local,
        mesh=cut,
        in_specs=(P(rows, cols), P(None, cols, None), P(), P(None, every, None)),
        out_specs=(P(None, every, None), P(None, every, None)),
        check_vma=False,
    )
```

time: 81.1 us -> 72.5 us (0.89)
  local copies, waits for them, and re-layouts: 10.2 us -> 0.68 us
  starting transfers between devices: 26.1 us -> 32.5 us
  waiting for transfers between devices: 30.1 us -> 27 us
  other arithmetic: 1.99 us -> 0.69 us
  Pallas kernels: 11.7 us -> 10.6 us
    all_to_all x1 -> x2, starting transfers between devices: 10.7 us -> 18.3 us  [the longest x1 9.16 us: local(): pieces = lax.all_to_all(g, ('x', 'y'), 0, 0, tiled=True)]
    unnamed x14 -> x4, local copies, waits for them, and re-layouts: 7.59 us -> 0.68 us
    ppermute x3, waiting for transfers between devices: 13 us -> 10.6 us  [local(): arrived = [lax.ppermute(sent[m - 1], 'zl', xor4[m]) for m in (3, 2, 1)]]
    squeeze x1 -> x0, local copies, waits for them, and re-layouts: 1.59 us -> none  [local(): lax.dynamic_slice(panel, (x & 1, y * height + (2 * zh + (x >> 1)) * part,...]
    ppermute x1, starting transfers between devices: 2.23 us -> 0.94 us  [local(): off_other = lax.ppermute(off_send, 'c', swap)]
    pallas_call x1, Pallas kernels: 1.2 us -> 0.15 us  [join(): pl.pallas_call(kernel, in_specs=[scalars(), whole(), whole()], out_specs=...]
    reshape x1 -> x0, local copies, waits for them, and re-layouts: 0.99 us -> none  [local(): pieces = lax.all_to_all(g.reshape(256, 2, wide), every, 0, 0, tiled=True)]
    ppermute x1, waiting for transfers between devices: 0.92 us -> 0.01 us  [local(): off_other = lax.ppermute(off_send, 'c', swap)]
  transfers between devices with their start and end apart: 7 -> 8, of which waited for: 4 -> 4; matrix products, arithmetic and copies ran while one was open for 3% -> 1% of each run, Pallas kernels for 7% -> 1%
where the time goes in v2:
time: 72.5 us; the launch traced here: 72.2 us
  starting transfers between devices  32.5 us (45%)
  waiting for transfers between devices  27 us (37%)
  Pallas kernels  10.6 us (15%)
    ppermute x3, waiting for transfers between devices, local(): arrived = [lax.ppermute(sent[m - 1], 'zl', xor4[m]) for m in (3, 2, 1)]  10.6 us
    all_to_all x1, waiting for transfers between devices, local(): pieces = lax.all_to_all(g, ('x', 'y'), 0, 0, tiled=True)  9.36 us
    all_to_all x1, starting transfers between devices, local(): pieces = lax.all_to_all(g, ('x', 'y'), 0, 0, tiled=True)  9.16 us
    all_to_all x1, starting transfers between devices, local(): pieces = lax.all_to_all(gather(pieces), ('zh', 'zl', 'c'), 0, 0, tiled=True)  9.14 us
    ppermute x3, starting transfers between devices, local(): arrived = [lax.ppermute(sent[m - 1], 'zl', xor4[m]) for m in (3, 2, 1)]  8.02 us
    pallas_call x1, Pallas kernels, products(): pl.pallas_call(kernel, in_specs=[scalars(), hbm(), hbm(), hbm()], out_spe...  7.91 us
    all_to_all x1, waiting for transfers between devices, local(): pieces = lax.all_to_all(gather(pieces), ('zh', 'zl', 'c'), 0, 0, tiled=True)  7.11 us
    ppermute x1, starting transfers between devices, local(): swapped = lax.ppermute(other, 'c', swap)  3.33 us
  transfers between devices with their start and end apart: 8, of which 4 were waited for; matrix products, arithmetic and copies ran while one was open for 1% of the time, Pallas kernels for 1%

profile of v2, /device:TPU:1, one launch (start us, length us, event | category | flops | bytes accessed | tf_op | source)
XLA Modules:
  0.0 72.2 jit_solution(30327528983233699)
XLA Ops:
  0.7 0.7 copy-done.1
  1.3 7.9 %products.1 = (bf16[640,512]{1,0:T(8,128)(2,1)S(1)}, f32[640,512]{1,0:T(8,128)S(1)}, bf16[160,512]{1,0:T(8,128)(2,1)S(1)}) custom-call(s32[1]{0:T(128)} %bitcast.me_ref, bf16[640,2560]{1,0:T(8,128)(2,1)} %a_hbm.1, bf16[2,2560,512]{2,1,0:T(8,128)(2,1)} %l_hbm.1, s32[2,80]{1,0:T(2,128)S(1)} %copy-done.1), custom_call_target="tpu_custom_call" | custom-call | flops 3355443200 | bytes 9830400 | tf_op jit(solution)/shard_map/products/pallas_call | solution.py:101
  9.2 0.0 copy-start
  9.3 3.3 %collective-permute-start.1 = (bf16[640,512]{1,0:T(8,128)(2,1)S(1)}, bf16[640,512]{1,0:T(8,128)(2,1)S(1)}, u32[]{:S(2)}, u32[]{:S(2)}) collective-permute-start(bf16[640,512]{1,0:T(8,128)(2,1)S(1)} %get-tuple-element.14), channel_id=1, source_target_pairs={{0,1},{1,0},{2,3},{3,2},{4,5},{5,4},{6,7},{7,6},{8,9},{9,8},{10,11... | collective-permute-start | bytes 1966088 | tf_op jit(solution)/shard_map/ppermute | solution.py:244
  12.6 1.9 %collective-permute-start = (bf16[160,512]{1,0:T(8,128)(2,1)S(1)}, bf16[160,512]{1,0:T(8,128)(2,1)S(1)}, u32[]{:S(2)}, u32[]{:S(2)}) collective-permute-start(bf16[160,512]{1,0:T(8,128)(2,1)S(1)} %get-tuple-element.12), channel_id=1, source_target_pairs={{0,0},{1,32},{2,64},{3,96},{4,128},{5,160},{6,192},{7,224},{8,8},{... | collective-permute-start | bytes 491528 | tf_op jit(solution)/shard_map/ppermute | solution.py:245
  14.5 0.0 collective-permute-done.1.in_ref
  14.5 0.1 join.1
  14.7 7.6 %collective-permute-start.2 = (bf16[160,512]{1,0:T(8,128)(2,1)S(1)}, bf16[160,512]{1,0:T(8,128)(2,1)S(1)}, u32[]{:S(2)}, u32[]{:S(2)}) collective-permute-start(bf16[160,512]{1,0:T(8,128)(2,1)S(1)} %get-tuple-element.16), channel_id=1, source_target_pairs={{0,6},{2,4},{4,2},{6,0},{1,7},{3,5},{5,3},{7,1},{8,14},{10,12},{12... | collective-permute-start | bytes 491528 | tf_op jit(solution)/shard_map/ppermute | solution.py:247
  22.3 0.0 collective-permute-start.3
  22.3 0.4 collective-permute-start.4
  22.7 0.0 collective-permute-done.m_ref
  22.7 8.9 %collective-permute-done.2.rest_0_ = bf16[160,512]{1,0:T(8,128)(2,1)S(1)} collective-permute-done((bf16[160,512]{1,0:T(8,128)(2,1)S(1)}, bf16[160,512]{1,0:T(8,128)(2,1)S(1)}, u32[]{:S(2)}, u32[]{:S(2)}) %collective-permute-start.2) | collective-permute-done | bytes 163872 | tf_op jit(solution)/shard_map/ppermute | solution.py:247
  31.6 0.0 collective-permute-done.3.rest_1_
  31.6 1.6 %collective-permute-done.4.rest_2_ = bf16[160,512]{1,0:T(8,128)(2,1)S(1)} collective-permute-done((bf16[160,512]{1,0:T(8,128)(2,1)S(1)}, bf16[160,512]{1,0:T(8,128)(2,1)S(1)}, u32[]{:S(2)}, u32[]{:S(2)}) %collective-permute-start.4) | collective-permute-done | bytes 163872 | tf_op jit(solution)/shard_map/ppermute | solution.py:247
  33.2 1.2 %contract.1 = (bf16[80,512]{1,0:T(8,128)(2,1)S(1)}, bf16[80,512]{1,0:T(8,128)(2,1)S(1)}, bf16[16,32,512]{2,1,0:T(8,128)(2,1)}) custom-call(s32[1]{0:T(128)} %bitcast.me_ref, s32[2,80]{1,0:T(2,128)S(1)} %copy-done.1, bf16[160,512]{1,0:T(8,128)(2,1)S(1)} %collective-permute-done.m_ref, f32[160,512]{1,0:T(8,128)S(1)} %get-tuple-element.15.keep_ref, ...), custom_call_target="tpu_custom_call" | custom-call | tf_op jit(solution)/shard_map/contract/pallas_call | solution.py:178
  34.5 9.2 %all-to-all-start = ((bf16[16,32,512]{2,1,0:T(8,128)(2,1)}), bf16[16,32,512]{2,1,0:T(8,128)(2,1)S(1)}, u32[]{:S(2)}, u32[]{:S(2)}) async-start(bf16[16,32,512]{2,1,0:T(8,128)(2,1)} %get-tuple-element.21), calls=%async_computation | async-start | bytes 1048576 | tf_op jit(solution)/shard_map/all_to_all | solution.py:249
  43.7 0.9 %collective-permute-start.5 = (bf16[80,512]{1,0:T(8,128)(2,1)S(1)}, bf16[80,512]{1,0:T(8,128)(2,1)S(1)}, u32[]{:S(2)}, u32[]{:S(2)}) collective-permute-start(bf16[80,512]{1,0:T(8,128)(2,1)S(1)} %get-tuple-element.20), channel_id=1, source_target_pairs={{0,1},{1,0},{2,3},{3,2},{4,5},{5,4},{6,7},{7,6},{8,9},{9,8},{10,11... | collective-permute-start | bytes 245768 | tf_op jit(solution)/shard_map/ppermute | solution.py:250
  44.6 9.4 %all-to-all-done.in_ref = bf16[16,32,512]{2,1,0:T(8,128)(2,1)S(1)} async-done(((bf16[16,32,512]{2,1,0:T(8,128)(2,1)}), bf16[16,32,512]{2,1,0:T(8,128)(2,1)S(1)}, u32[]{:S(2)}, u32[]{:S(2)}) %all-to-all-start) | async-done | bytes 524320 | tf_op jit(solution)/shard_map/all_to_all | solution.py:249
  54.0 0.7 gather.1
  54.7 9.1 %all-to-all-start.1 = ((f32[16,2,512]{2,1,0:T(2,128)}), f32[16,2,512]{2,1,0:T(2,128)S(1)}, u32[]{:S(2)}, u32[]{:S(2)}) async-start(f32[16,2,512]{2,1,0:T(2,128)} %gather.1), calls=%async_computation.1 | async-start | bytes 131072 | tf_op jit(solution)/shard_map/all_to_all | solution.py:252
  63.8 0.0 collective-permute-done.5
  63.8 0.7 maximum_select_fusion
  64.5 7.1 %all-to-all-done.1.in_ref = f32[16,2,512]{2,1,0:T(2,128)S(1)} async-done(((f32[16,2,512]{2,1,0:T(2,128)}), f32[16,2,512]{2,1,0:T(2,128)S(1)}, u32[]{:S(2)}, u32[]{:S(2)}) %all-to-all-start.1) | async-done | bytes 65568 | tf_op jit(solution)/shard_map/all_to_all | solution.py:252
  71.6 0.6 finish.1
  (2 shorter events, 0.0 us)
Async XLA Ops:
  0.6 0.7 copy-start.1
  9.2 62.4 %copy-start = (f32[2,2,512]{2,1,0:T(2,128)S(1)}, f32[2,2,512]{2,1,0:T(2,128)}, u32[]{:S(2)}) copy-start(f32[2,2,512]{2,1,0:T(2,128)} %d_ref.1) | copy-start | bytes 24580
  9.3 5.2 %collective-permute-start.1 = (bf16[640,512]{1,0:T(8,128)(2,1)S(1)}, bf16[640,512]{1,0:T(8,128)(2,1)S(1)}, u32[]{:S(2)}, u32[]{:S(2)}) collective-permute-start(bf16[640,512]{1,0:T(8,128)(2,1)S(1)} %get-tuple-element.14), channel_id=1, source_target_pairs={{0,1},{1,0},{2,3},{3,2},{4,5},{5,4},{6,7},{7,6},{8,9},{9,8},{10,11... | collective-permute-start | bytes 1966088 | tf_op jit(solution)/shard_map/ppermute | solution.py:244
  12.6 10.1 %collective-permute-start = (bf16[160,512]{1,0:T(8,128)(2,1)S(1)}, bf16[160,512]{1,0:T(8,128)(2,1)S(1)}, u32[]{:S(2)}, u32[]{:S(2)}) collective-permute-start(bf16[160,512]{1,0:T(8,128)(2,1)S(1)} %get-tuple-element.12), channel_id=1, source_target_pairs={{0,0},{1,32},{2,64},{3,96},{4,128},{5,160},{6,192},{7,224},{8,8},{... | collective-permute-start | bytes 491528 | tf_op jit(solution)/shard_map/ppermute | solution.py:245
  14.7 16.9 %collective-permute-start.2 = (bf16[160,512]{1,0:T(8,128)(2,1)S(1)}, bf16[160,512]{1,0:T(8,128)(2,1)S(1)}, u32[]{:S(2)}, u32[]{:S(2)}) collective-permute-start(bf16[160,512]{1,0:T(8,128)(2,1)S(1)} %get-tuple-element.16), channel_id=1, source_target_pairs={{0,6},{2,4},{4,2},{6,0},{1,7},{3,5},{5,3},{7,1},{8,14},{10,12},{12... | collective-permute-start | bytes 491528 | tf_op jit(solution)/shard_map/ppermute | solution.py:247
  22.3 9.3 %collective-permute-start.3 = (bf16[160,512]{1,0:T(8,128)(2,1)S(1)}, bf16[160,512]{1,0:T(8,128)(2,1)S(1)}, u32[]{:S(2)}, u32[]{:S(2)}) collective-permute-start(bf16[160,512]{1,0:T(8,128)(2,1)S(1)} %get-tuple-element.17), channel_id=1, source_target_pairs={{0,4},{2,6},{4,0},{6,2},{1,5},{3,7},{5,1},{7,3},{8,12},{10,14},{12... | collective-permute-start | bytes 491528 | tf_op jit(solution)/shard_map/ppermute | solution.py:247
  22.3 10.9 %collective-permute-start.4 = (bf16[160,512]{1,0:T(8,128)(2,1)S(1)}, bf16[160,512]{1,0:T(8,128)(2,1)S(1)}, u32[]{:S(2)}, u32[]{:S(2)}) collective-permute-start(bf16[160,512]{1,0:T(8,128)(2,1)S(1)} %get-tuple-element.18), channel_id=1, source_target_pairs={{0,2},{2,0},{4,6},{6,4},{1,3},{3,1},{5,7},{7,5},{8,10},{10,8},{12,... | collective-permute-start | bytes 491528 | tf_op jit(solution)/shard_map/ppermute | solution.py:247
  34.5 19.5 %all-to-all-start = ((bf16[16,32,512]{2,1,0:T(8,128)(2,1)}), bf16[16,32,512]{2,1,0:T(8,128)(2,1)S(1)}, u32[]{:S(2)}, u32[]{:S(2)}) async-start(bf16[16,32,512]{2,1,0:T(8,128)(2,1)} %get-tuple-element.21), calls=%async_computation | async-start | bytes 1048576 | tf_op jit(solution)/shard_map/all_to_all | solution.py:249
  43.7 20.1 %collective-permute-start.5 = (bf16[80,512]{1,0:T(8,128)(2,1)S(1)}, bf16[80,512]{1,0:T(8,128)(2,1)S(1)}, u32[]{:S(2)}, u32[]{:S(2)}) collective-permute-start(bf16[80,512]{1,0:T(8,128)(2,1)S(1)} %get-tuple-element.20), channel_id=1, source_target_pairs={{0,1},{1,0},{2,3},{3,2},{4,5},{5,4},{6,7},{7,6},{8,9},{9,8},{10,11... | collective-permute-start | bytes 245768 | tf_op jit(solution)/shard_map/ppermute | solution.py:250
  54.7 17.0 %all-to-all-start.1 = ((f32[16,2,512]{2,1,0:T(2,128)}), f32[16,2,512]{2,1,0:T(2,128)S(1)}, u32[]{:S(2)}, u32[]{:S(2)}) async-start(f32[16,2,512]{2,1,0:T(2,128)} %gather.1), calls=%async_computation.1 | async-start | bytes 131072 | tf_op jit(solution)/shard_map/all_to_all | solution.py:252

commit v3 on v2

--- a/solution.py
+++ b/solution.py
@@ -43,6 +43,16 @@
 
 STEP = 512
 LIMIT = 50
+ROUTES = (
+    (1, 4, 2, 3, 7, 6, 5, 0),
+    (4, 3, 2, 1, 0, 5, 7, 6),
+    (3, 5, 4, 2, 7, 0, 6, 1),
+    (4, 2, 3, 5, 1, 6, 0, 7),
+    (1, 7, 6, 0, 2, 5, 4, 3),
+    (7, 1, 0, 6, 4, 2, 3, 5),
+    (0, 2, 6, 1, 5, 4, 7, 3),
+    (1, 7, 0, 2, 6, 3, 5, 4),
+)
 
 
 def cost(height, breadth, wide):
@@ -57,9 +67,8 @@
     height, breadth = ancestor.shape
     wide = panel.shape[2]
     steps = breadth // STEP
-    part = height // 4
-
-    def kernel(me_ref, a_hbm, l_hbm, p_hbm, o_ref, k_ref, f_ref, p_ref, a_buf, l_buf, acc, a_sem, l_sem, f_sem, p_sem):
+
+    def kernel(me_ref, a_hbm, l_hbm, p_hbm, o_ref, k_ref, p_ref, a_buf, l_buf, acc, a_sem, l_sem, p_sem):
         zh, x, y, zl, c = place_of(me_ref[0])
         listed = pltpu.make_async_copy(p_hbm, p_ref, p_sem)
         listed.start()
@@ -77,9 +86,6 @@
             a_copies[k].start()
             l_copies[k][0].start()
             l_copies[k][1].start()
-        start = pl.multiple_of(y * height + (2 * zh + (x >> 1)) * part, 16)
-        fetch = pltpu.make_async_copy(l_hbm.at[x & 1, pl.ds(start, part), :], f_ref, f_sem)
-        fetch.start()
         listed.wait()
         first = (zl * 2 + c) * (breadth // BLOCK)
         for k in range(steps):
@@ -96,16 +102,14 @@
                     o_ref[...] = (total[...] + term).astype(BF16)
                 else:
                     total[...] += term
-        fetch.wait()
 
     return pl.pallas_call(
         kernel,
         in_specs=[scalars(), hbm(), hbm(), hbm()],
-        out_specs=[whole(), whole(), whole()],
+        out_specs=[whole(), whole()],
         out_shape=[
             jax.ShapeDtypeStruct((height, wide), BF16),
             jax.ShapeDtypeStruct((height, wide), F32),
-            jax.ShapeDtypeStruct((part, wide), BF16),
         ],
         scratch_shapes=[
             pltpu.VMEM(pattern.shape, pattern.dtype),
@@ -115,7 +119,6 @@
             pltpu.SemaphoreType.DMA((steps,)),
             pltpu.SemaphoreType.DMA((2, steps)),
             pltpu.SemaphoreType.DMA,
-            pltpu.SemaphoreType.DMA,
         ],
         compiler_params=params(LIMIT),
         cost_estimate=cost(height, breadth, 2 * wide),
@@ -123,50 +126,88 @@
     )(me, ancestor, panel, pattern)
 
 
-def join(me, own, arrived, lines):
+def pick(me, height, panel):
+    part, wide = height // 4, panel.shape[2]
+
+    def kernel(me_ref, l_hbm, f_ref, sem):
+        zh, x, y, zl, c = place_of(me_ref[0])
+        code = jnp.int32(0)
+        for p, row in enumerate(ROUTES):
+            code = jnp.where(zl * 2 + c == p, sum(v << (3 * q) for q, v in enumerate(row)), code)
+        to = (code >> (3 * (zh * 4 + x))) & 7
+        copies = []
+        for m in range(2):
+            start = pl.multiple_of(y * height + ((to >> 1) ^ (2 * m)) * part, 16)
+            copies.append(
+                pltpu.make_async_copy(
+                    l_hbm.at[to & 1, pl.ds(start, part), :], f_ref.at[pl.ds(m * part, part), :], sem.at[m]
+                )
+            )
+            copies[m].start()
+        for copy in copies:
+            copy.wait()
+
+    return pl.pallas_call(
+        kernel,
+        in_specs=[scalars(), hbm()],
+        out_specs=hbm(),
+        out_shape=jax.ShapeDtypeStruct((2 * part, wide), panel.dtype),
+        scratch_shapes=[pltpu.SemaphoreType.DMA((2,))],
+        compiler_params=params(LIMIT),
+        name="pick",
+    )(me, panel)
+
+
+def join(me, own, arrived):
     height, wide = own.shape
-    part = height // lines
-
-    def kernel(me_ref, own_ref, in_ref, keep_ref, *sent):
+    part = height // 4
+
+    def kernel(me_ref, own_ref, in_ref, near_ref, far_ref, sent_ref):
         here = place_of(me_ref[0])[3]
-        for m in range(lines):
+        for m in range(4):
             rows = pl.ds(pl.multiple_of((here ^ m) * part, 16), part)
             total = own_ref[rows, :] + in_ref[rows, :].astype(F32)
             if m == 0:
-                keep_ref[...] = total
+                near_ref[...] = total
+            elif m == 2:
+                far_ref[...] = total
             else:
-                sent[m - 1][...] = total.astype(BF16)
-
-    piece = jax.ShapeDtypeStruct((part, wide), BF16)
+                sent_ref[(m // 2) * part : (m // 2 + 1) * part, :] = total.astype(BF16)
+
+    piece = jax.ShapeDtypeStruct((part, wide), F32)
     return pl.pallas_call(
         kernel,
         in_specs=[scalars(), whole(), whole()],
-        out_specs=[whole()] * lines,
-        out_shape=[jax.ShapeDtypeStruct((part, wide), F32)] + [piece] * (lines - 1),
+        out_specs=[whole()] * 3,
+        out_shape=[piece, piece, jax.ShapeDtypeStruct((2 * part, wide), BF16)],
         compiler_params=params(),
         name="join",
     )(me, own, arrived)
 
 
-def contract(me, height, pattern, mine, keep, arrived):
-    part, wide = keep.shape
-    half = part // 2
-
-    def kernel(me_ref, p_ref, m_ref, keep_ref, *rest):
+def chosen(first, count, pattern_row):
+    ids = (first + lax.broadcasted_iota(jnp.int32, (count, 1), 0)) >> 7
+    return jnp.max(jnp.where(ids == pattern_row, 1.0, 0.0).astype(F32), axis=1, keepdims=True)
+
+
+def contract(me, height, pattern, mine, near, far, arrived):
+    part, wide = near.shape
+
+    def kernel(me_ref, p_ref, m_ref, near_ref, far_ref, in_ref, half_ref, sent_ref, g_ref, m_buf, s_buf):
         zh, x, y, zl, core = place_of(me_ref[0])
-        first = ((zh * 4 + x) * 4 + y) * height + zl * part
-        ins, (own_ref, send_ref, g_ref, off) = rest[: len(arrived)], rest[len(arrived) :]
-        total = keep_ref[...]
-        for r in ins:
-            total = total + r[...].astype(F32)
         row = p_ref[pl.ds(core, 1), :]
-        ids = (first + lax.broadcasted_iota(jnp.int32, (part, 1), 0)) >> 7
-        hit = jnp.max(jnp.where(ids == row, 1.0, 0.0).astype(F32), axis=1, keepdims=True)
-        off[...] = -(total * hit)
-        own_ref[...] = off[pl.ds(pl.multiple_of(core * half, 16), half), :].astype(BF16)
-        send_ref[...] = off[pl.ds(pl.multiple_of((1 - core) * half, 16), half), :].astype(BF16)
-        chosen = m_ref[...] * hit.astype(BF16)
-        g = lax.dot_general(chosen, total.astype(BF16), (((0,), (0,)), ((), ())), preferred_element_type=F32)
+        base = ((zh * 4 + x) * 4 + y) * height
+        near_sum = near_ref[...] + in_ref[:part, :].astype(F32)
+        half_ref[...] = near_sum
+        far_sum = (far_ref[...] + in_ref[part:, :].astype(F32)).astype(BF16)
+        sent_ref[...] = far_sum
+        s_buf[:part, :] = near_sum.astype(BF16)
+        s_buf[part:, :] = far_sum
+        for m in range(2):
+            hit = chosen(base + (zl ^ (2 * m)) * part, part, row)
+            rows = slice(m * part, (m + 1) * part)
+            m_buf[rows, :] = m_ref[rows, :] * hit.astype(BF16)
+        g = lax.dot_general(m_buf[...], s_buf[...], (((0,), (0,)), ((), ())), preferred_element_type=F32)
         g = g.astype(BF16)
         groups, both = g_ref.shape[0], g_ref.shape[1] // 2
         for i in range(groups):
@@ -174,16 +215,42 @@
                 start = h * (wide // 2) + i * both
                 g_ref[i, h * both : (h + 1) * both, :] = g[start : start + both, :]
 
-    piece = jax.ShapeDtypeStruct((half, wide), BF16)
-    return pl.pallas_call(
-        kernel,
-        in_specs=[scalars()] + [whole()] * (3 + len(arrived)),
+    return pl.pallas_call(
+        kernel,
+        in_specs=[scalars()] + [whole()] * 5,
         out_specs=[whole()] * 3,
-        out_shape=[piece, piece, jax.ShapeDtypeStruct((16, wide // 16, wide), BF16)],
+        out_shape=[
+            jax.ShapeDtypeStruct((part, wide), F32),
+            jax.ShapeDtypeStruct((part, wide), BF16),
+            jax.ShapeDtypeStruct((16, wide // 16, wide), BF16),
+        ],
+        scratch_shapes=[pltpu.VMEM((2 * part, wide), BF16), pltpu.VMEM((2 * part, wide), BF16)],
+        compiler_params=params(),
+        name="contract",
+    )(me, pattern, mine, near, far, arrived)
+
+
+def negate(me, height, pattern, half, arrived):
+    part, wide = half.shape
+    each = part // 2
+
+    def kernel(me_ref, p_ref, half_ref, in_ref, own_ref, send_ref, off):
+        zh, x, y, zl, core = place_of(me_ref[0])
+        hit = chosen(((zh * 4 + x) * 4 + y) * height + zl * part, part, p_ref[pl.ds(core, 1), :])
+        off[...] = -((half_ref[...] + in_ref[...].astype(F32)) * hit)
+        own_ref[...] = off[pl.ds(pl.multiple_of(core * each, 16), each), :].astype(BF16)
+        send_ref[...] = off[pl.ds(pl.multiple_of((1 - core) * each, 16), each), :].astype(BF16)
+
+    piece = jax.ShapeDtypeStruct((each, wide), BF16)
+    return pl.pallas_call(
+        kernel,
+        in_specs=[scalars()] + [whole()] * 3,
+        out_specs=[whole()] * 2,
+        out_shape=[piece, piece],
         scratch_shapes=[pltpu.VMEM((part, wide), F32)],
         compiler_params=params(),
-        name="contract",
-    )(me, pattern, mine, keep, *arrived)
+        name="negate",
+    )(me, pattern, half, arrived)
 
 
 def gather(pieces):
@@ -227,26 +294,26 @@
 def solution(mesh):
     cut = Mesh(mesh.devices.reshape(2, 4, 4, 4, 2), ("zh", "x", "y", "zl", "c"))
     every = ("zh", "x", "y", "zl", "c")
-    xor4 = {m: [(i, i ^ m) for i in range(4)] for m in (1, 2, 3)}
+    xor4 = {m: [(i, i ^ m) for i in range(4)] for m in (1, 2)}
     swap = [(0, 1), (1, 0)]
     fetch = []
-    for zh in range(2):
-        for x in range(4):
-            for y in range(4):
-                for p in range(8):
-                    source = ((zh * 4 + x) * 4 + y) * 8 + p
-                    fetch.append((source, (p * 4 + y) * 8 + (2 * zh + (x >> 1)) * 2 + (x & 1)))
+    for source in range(256):
+        zh, x, y, p = source >> 7, (source >> 5) & 3, (source >> 3) & 3, source & 7
+        fetch.append((source, (p * 4 + y) * 8 + ROUTES[p][zh * 4 + x]))
 
     def local(ancestor, panel, pattern, diag):
         me = jnp.reshape(lax.axis_index(every), (1,))
         core = lax.axis_index("c")
-        other, own, fetched = products(me, ancestor, panel, pattern)
+        height = ancestor.shape[0]
+        mine = lax.ppermute(pick(me, height, panel), every, fetch)
+        other, own = products(me, ancestor, panel, pattern)
         swapped = lax.ppermute(other, "c", swap)
-        mine = lax.ppermute(fetched, every, fetch)
-        keep, *sent = join(me, own, swapped, 4)
-        arrived = [lax.ppermute(sent[m - 1], "zl", xor4[m]) for m in (3, 2, 1)]
-        off_own, off_send, g = contract(me, ancestor.shape[0], pattern, mine, keep, arrived)
+        near, far, sent = join(me, own, swapped)
+        arrived = lax.ppermute(sent, "zl", xor4[1])
+        half, sent, g = contract(me, height, pattern, mine, near, far, arrived)
+        arrived = lax.ppermute(sent, "zl", xor4[2])
         pieces = lax.all_to_all(g, ("x", "y"), 0, 0, tiled=True)
+        off_own, off_send = negate(me, height, pattern, half, arrived)
         off_other = lax.ppermute(off_send, "c", swap)
         off = jnp.where(core == 0, jnp.stack([off_own, off_other]), jnp.stack([off_other, off_own]))
         pieces = lax.all_to_all(gather(pieces), ("zh", "zl", "c"), 0, 0, tiled=True)

time: 72.5 us -> 66.5 us (0.917)
  starting transfers between devices: 32.5 us -> 26.4 us
  Pallas kernels: 10.6 us -> 11.8 us
  waiting for transfers between devices: 27 us -> 25.9 us
    all_to_all x1, waiting for transfers between devices: 9.36 us -> 0.01 us  [local(): pieces = lax.all_to_all(g, ('x', 'y'), 0, 0, tiled=True)]
    ppermute x4 -> x3, waiting for transfers between devices: 10.6 us -> 18.8 us  [the longest x1 7.45 us: local(): arrived = lax.ppermute(sent, 'zl', xor4[2])]
    all_to_all x1, starting transfers between devices: 9.16 us -> 6.21 us  [local(): pieces = lax.all_to_all(g, ('x', 'y'), 0, 0, tiled=True)]
    all_to_all x1, starting transfers between devices: 9.14 us -> 6.46 us  [local(): pieces = lax.all_to_all(gather(pieces), ('zh', 'zl', 'c'), 0, 0, tiled=True)]
    pallas_call x1 -> x3, Pallas kernels: 1.24 us -> 2.51 us  [the longest x1 1.36 us: contract(): pl.pallas_call(kernel, in_specs=[scalars()] + [whole()] * 5, out_specs=[w...]
    ppermute x4 -> x3, starting transfers between devices: 9.93 us -> 9.84 us  [the longest x1 6.02 us: local(): arrived = lax.ppermute(sent, 'zl', xor4[2])]
  transfers between devices with their start and end apart: 8 -> 7, of which waited for: 4 -> 4; matrix products, arithmetic and copies ran while one was open for 1% -> 1% of each run, Pallas kernels for 1% -> 3%
where the time goes in v3:
time: 66.5 us; the launch traced here: 66.2 us
  starting transfers between devices  26.4 us (40%)
  waiting for transfers between devices  25.9 us (39%)
  Pallas kernels  11.8 us (18%)
  between operations  0.71 us (1%)
  local copies, waits for them, and re-layouts  0.69 us (1%)
  other arithmetic  0.69 us (1%)
    pallas_call x1, Pallas kernels, products(): pl.pallas_call(kernel, in_specs=[scalars(), hbm(), hbm(), hbm()], out_spe...  7.9 us
    ppermute x1, waiting for transfers between devices, local(): arrived = lax.ppermute(sent, 'zl', xor4[2])  7.45 us
    ppermute x1, waiting for transfers between devices, local(): arrived = lax.ppermute(sent, 'zl', xor4[1])  7.24 us
    all_to_all x1, waiting for transfers between devices, local(): pieces = lax.all_to_all(gather(pieces), ('zh', 'zl', 'c'), 0, 0, tiled=True)  7.12 us
    all_to_all x1, starting transfers between devices, local(): pieces = lax.all_to_all(gather(pieces), ('zh', 'zl', 'c'), 0, 0, tiled=True)  6.46 us
    all_to_all x1, starting transfers between devices, local(): pieces = lax.all_to_all(g, ('x', 'y'), 0, 0, tiled=True)  6.21 us
    ppermute x1, starting transfers between devices, local(): arrived = lax.ppermute(sent, 'zl', xor4[2])  6.02 us
    ppermute x1, waiting for transfers between devices, local(): mine = lax.ppermute(pick(me, height, panel), every, fetch)  4.11 us
  transfers between devices with their start and end apart: 7, of which 4 were waited for; matrix products, arithmetic and copies ran while one was open for 1% of the time, Pallas kernels for 3%

profile of v3, /device:TPU:1, one launch (start us, length us, event | category | flops | bytes accessed | tf_op | source)
XLA Modules:
  0.0 66.2 jit_solution(1568786299778158021)
XLA Ops:
  0.6 0.0 copy-start.1
  0.7 0.7 %copy-done.1 = s32[2,80]{1,0:T(2,128)S(1)} copy-done((s32[2,80]{1,0:T(2,128)S(1)}, s32[2,80]{1,0:T(2,128)}, u32[]{:S(2)}) %copy-start.1) | copy-done | bytes 664
  1.3 7.9 %products.1 = (bf16[640,512]{1,0:T(8,128)(2,1)S(1)}, f32[640,512]{1,0:T(8,128)S(1)}) custom-call(s32[1]{0:T(128)} %bitcast.me_ref, bf16[640,2560]{1,0:T(8,128)(2,1)} %a_hbm.1, bf16[2,2560,512]{2,1,0:T(8,128)(2,1)} %l_hbm.3, s32[2,80]{1,0:T(2,128)S(1)} %copy-done.1), custom_call_target="tpu_custom_call" | custom-call | flops 3355443200 | bytes 9830400 | tf_op jit(solution)/shard_map/products/pallas_call | solution.py:106
  9.2 0.0 copy-start.2
  9.2 3.3 %collective-permute-start.1 = (bf16[640,512]{1,0:T(8,128)(2,1)S(1)}, bf16[640,512]{1,0:T(8,128)(2,1)S(1)}, u32[]{:S(2)}, u32[]{:S(2)}) collective-permute-start(bf16[640,512]{1,0:T(8,128)(2,1)S(1)} %get-tuple-element.13), channel_id=1, source_target_pairs={{0,1},{1,0},{2,3},{3,2},{4,5},{5,4},{6,7},{7,6},{8,9},{9,8},{10,11... | collective-permute-start | bytes 1966088 | tf_op jit(solution)/shard_map/ppermute | solution.py:310
  12.6 1.0 %pick.1 = bf16[320,512]{1,0:T(8,128)(2,1)S(1)} custom-call(s32[1]{0:T(128)} %bitcast.me_ref, bf16[2,2560,512]{2,1,0:T(8,128)(2,1)} %l_hbm.3), custom_call_target="tpu_custom_call" | custom-call | tf_op jit(solution)/shard_map/pick/pallas_call | solution.py:150
  13.6 0.0 copy-start
  13.6 2.2 %collective-permute-start = (bf16[320,512]{1,0:T(8,128)(2,1)S(1)}, bf16[320,512]{1,0:T(8,128)(2,1)S(1)}, u32[]{:S(2)}, u32[]{:S(2)}) collective-permute-start(bf16[320,512]{1,0:T(8,128)(2,1)S(1)} %pick.1), channel_id=1, source_target_pairs={{0,1},{1,36},{2,67},{3,100},{4,129},{5,167},{6,192},{7,225},{8,9},... | collective-permute-start | bytes 983048 | tf_op jit(solution)/shard_map/ppermute | solution.py:308
  15.8 0.0 collective-permute-done.1.in_ref
  15.8 0.1 join.1
  15.9 1.6 %collective-permute-start.2 = (bf16[320,512]{1,0:T(8,128)(2,1)S(1)}, bf16[320,512]{1,0:T(8,128)(2,1)S(1)}, u32[]{:S(2)}, u32[]{:S(2)}) collective-permute-start(bf16[320,512]{1,0:T(8,128)(2,1)S(1)} %get-tuple-element.16), channel_id=1, source_target_pairs={{0,2},{2,0},{4,6},{6,4},{1,3},{3,1},{5,7},{7,5},{8,10},{10,8},{12,... | collective-permute-start | bytes 983048 | tf_op jit(solution)/shard_map/ppermute | solution.py:312
  17.5 4.1 %collective-permute-done.m_ref = bf16[320,512]{1,0:T(8,128)(2,1)S(1)} collective-permute-done((bf16[320,512]{1,0:T(8,128)(2,1)S(1)}, bf16[320,512]{1,0:T(8,128)(2,1)S(1)}, u32[]{:S(2)}, u32[]{:S(2)}) %collective-permute-start) | collective-permute-done | bytes 327712 | tf_op jit(solution)/shard_map/ppermute | solution.py:308
  21.7 7.2 %collective-permute-done.2.in_ref = bf16[320,512]{1,0:T(8,128)(2,1)S(1)} collective-permute-done((bf16[320,512]{1,0:T(8,128)(2,1)S(1)}, bf16[320,512]{1,0:T(8,128)(2,1)S(1)}, u32[]{:S(2)}, u32[]{:S(2)}) %collective-permute-start.2) | collective-permute-done | bytes 327712 | tf_op jit(solution)/shard_map/ppermute | solution.py:312
  28.9 1.4 %contract.1 = (f32[160,512]{1,0:T(8,128)S(1)}, bf16[160,512]{1,0:T(8,128)(2,1)S(1)}, bf16[16,32,512]{2,1,0:T(8,128)(2,1)}) custom-call(s32[1]{0:T(128)} %bitcast.me_ref, s32[2,80]{1,0:T(2,128)S(1)} %copy-done.2, bf16[320,512]{1,0:T(8,128)(2,1)S(1)} %collective-permute-done.m_ref, f32[160,512]{1,0:T(8,128)S(1)} %get-tuple-element.14.near_ref, ...), custom_call_target="tpu_custom_call" | custom-call | tf_op jit(solution)/shard_map/contract/pallas_call | solution.py:218
  30.3 6.2 %all-to-all-start = ((bf16[16,32,512]{2,1,0:T(8,128)(2,1)}), bf16[16,32,512]{2,1,0:T(8,128)(2,1)S(1)}, u32[]{:S(2)}, u32[]{:S(2)}) async-start(bf16[16,32,512]{2,1,0:T(8,128)(2,1)} %get-tuple-element.21), calls=%async_computation | async-start | bytes 1048576 | tf_op jit(solution)/shard_map/all_to_all | solution.py:315
  36.5 6.0 %collective-permute-start.3 = (bf16[160,512]{1,0:T(8,128)(2,1)S(1)}, bf16[160,512]{1,0:T(8,128)(2,1)S(1)}, u32[]{:S(2)}, u32[]{:S(2)}) collective-permute-start(bf16[160,512]{1,0:T(8,128)(2,1)S(1)} %get-tuple-element.18), channel_id=1, source_target_pairs={{0,4},{2,6},{4,0},{6,2},{1,5},{3,7},{5,1},{7,3},{8,12},{10,14},{12... | collective-permute-start | bytes 491528 | tf_op jit(solution)/shard_map/ppermute | solution.py:314
  42.5 7.4 %collective-permute-done.3.in_ref = bf16[160,512]{1,0:T(8,128)(2,1)S(1)} collective-permute-done((bf16[160,512]{1,0:T(8,128)(2,1)S(1)}, bf16[160,512]{1,0:T(8,128)(2,1)S(1)}, u32[]{:S(2)}, u32[]{:S(2)}) %collective-permute-start.3) | collective-permute-done | bytes 163872 | tf_op jit(solution)/shard_map/ppermute | solution.py:314
  49.9 0.1 negate.1
  50.1 0.6 collective-permute-start.4
  50.7 0.7 %gather.1 = f32[16,2,512]{2,1,0:T(2,128)} custom-call(bf16[16,32,512]{2,1,0:T(8,128)(2,1)S(1)} %all-to-all-done.in_ref), custom_call_target="tpu_custom_call" | custom-call | tf_op jit(solution)/shard_map/gather/pallas_call | solution.py:266
  51.4 6.5 %all-to-all-start.1 = ((f32[16,2,512]{2,1,0:T(2,128)}), f32[16,2,512]{2,1,0:T(2,128)S(1)}, u32[]{:S(2)}, u32[]{:S(2)}) async-start(f32[16,2,512]{2,1,0:T(2,128)} %gather.1), calls=%async_computation.1 | async-start | bytes 131072 | tf_op jit(solution)/shard_map/all_to_all | solution.py:319
  57.8 0.7 %maximum_select_fusion = bf16[2,80,512]{2,1,0:T(8,128)(2,1)} fusion(bf16[1,80,512]{2,1,0:T(8,128)(2,1)S(1)} %bitcast.4, bf16[1,80,512]{2,1,0:T(8,128)(2,1)S(1)} %bitcast.3, pred[]{:T(512)S(6)} %eq.3), kind=kLoop, calls=%fused_computation | loop fusion | flops 245760 | bytes 327681 | tf_op jit(solution)/shard_map/jit(_where)/select_n | solution.py:318
  58.5 7.1 %all-to-all-done.1.in_ref = f32[16,2,512]{2,1,0:T(2,128)S(1)} async-done(((f32[16,2,512]{2,1,0:T(2,128)}), f32[16,2,512]{2,1,0:T(2,128)S(1)}, u32[]{:S(2)}, u32[]{:S(2)}) %all-to-all-start.1) | async-done | bytes 65568 | tf_op jit(solution)/shard_map/all_to_all | solution.py:319
  65.6 0.6 finish.1
  (4 shorter events, 0.0 us)
Async XLA Ops:
  0.6 0.7 %copy-start.1 = (s32[2,80]{1,0:T(2,128)S(1)}, s32[2,80]{1,0:T(2,128)}, u32[]{:S(2)}) copy-start(s32[2,80]{1,0:T(2,128)} %p_ref.3) | copy-start | bytes 1924
  9.2 19.7 %copy-start.2 = (s32[2,80]{1,0:T(2,128)S(1)}, s32[2,80]{1,0:T(2,128)}, u32[]{:S(2)}) copy-start(s32[2,80]{1,0:T(2,128)} %p_ref.3) | copy-start | bytes 1924
  9.2 6.5 %collective-permute-start.1 = (bf16[640,512]{1,0:T(8,128)(2,1)S(1)}, bf16[640,512]{1,0:T(8,128)(2,1)S(1)}, u32[]{:S(2)}, u32[]{:S(2)}) collective-permute-start(bf16[640,512]{1,0:T(8,128)(2,1)S(1)} %get-tuple-element.13), channel_id=1, source_target_pairs={{0,1},{1,0},{2,3},{3,2},{4,5},{5,4},{6,7},{7,6},{8,9},{9,8},{10,11... | collective-permute-start | bytes 1966088 | tf_op jit(solution)/shard_map/ppermute | solution.py:310
  13.6 52.0 %copy-start = (f32[2,2,512]{2,1,0:T(2,128)S(1)}, f32[2,2,512]{2,1,0:T(2,128)}, u32[]{:S(2)}) copy-start(f32[2,2,512]{2,1,0:T(2,128)} %d_ref.1) | copy-start | bytes 24580
  13.6 8.0 %collective-permute-start = (bf16[320,512]{1,0:T(8,128)(2,1)S(1)}, bf16[320,512]{1,0:T(8,128)(2,1)S(1)}, u32[]{:S(2)}, u32[]{:S(2)}) collective-permute-start(bf16[320,512]{1,0:T(8,128)(2,1)S(1)} %pick.1), channel_id=1, source_target_pairs={{0,1},{1,36},{2,67},{3,100},{4,129},{5,167},{6,192},{7,225},{8,9},... | collective-permute-start | bytes 983048 | tf_op jit(solution)/shard_map/ppermute | solution.py:308
  15.9 13.0 %collective-permute-start.2 = (bf16[320,512]{1,0:T(8,128)(2,1)S(1)}, bf16[320,512]{1,0:T(8,128)(2,1)S(1)}, u32[]{:S(2)}, u32[]{:S(2)}) collective-permute-start(bf16[320,512]{1,0:T(8,128)(2,1)S(1)} %get-tuple-element.16), channel_id=1, source_target_pairs={{0,2},{2,0},{4,6},{6,4},{1,3},{3,1},{5,7},{7,5},{8,10},{10,8},{12,... | collective-permute-start | bytes 983048 | tf_op jit(solution)/shard_map/ppermute | solution.py:312
  30.3 20.4 %all-to-all-start = ((bf16[16,32,512]{2,1,0:T(8,128)(2,1)}), bf16[16,32,512]{2,1,0:T(8,128)(2,1)S(1)}, u32[]{:S(2)}, u32[]{:S(2)}) async-start(bf16[16,32,512]{2,1,0:T(8,128)(2,1)} %get-tuple-element.21), calls=%async_computation | async-start | bytes 1048576 | tf_op jit(solution)/shard_map/all_to_all | solution.py:315
  36.5 13.5 %collective-permute-start.3 = (bf16[160,512]{1,0:T(8,128)(2,1)S(1)}, bf16[160,512]{1,0:T(8,128)(2,1)S(1)}, u32[]{:S(2)}, u32[]{:S(2)}) collective-permute-start(bf16[160,512]{1,0:T(8,128)(2,1)S(1)} %get-tuple-element.18), channel_id=1, source_target_pairs={{0,4},{2,6},{4,0},{6,2},{1,5},{3,7},{5,1},{7,3},{8,12},{10,14},{12... | collective-permute-start | bytes 491528 | tf_op jit(solution)/shard_map/ppermute | solution.py:314
  50.1 7.7 %collective-permute-start.4 = (bf16[80,512]{1,0:T(8,128)(2,1)S(1)}, bf16[80,512]{1,0:T(8,128)(2,1)S(1)}, u32[]{:S(2)}, u32[]{:S(2)}) collective-permute-start(bf16[80,512]{1,0:T(8,128)(2,1)S(1)} %get-tuple-element.20), channel_id=1, source_target_pairs={{0,1},{1,0},{2,3},{3,2},{4,5},{5,4},{6,7},{7,6},{8,9},{9,8},{10,11... | collective-permute-start | bytes 245768 | tf_op jit(solution)/shard_map/ppermute | solution.py:317
  51.4 14.3 %all-to-all-start.1 = ((f32[16,2,512]{2,1,0:T(2,128)}), f32[16,2,512]{2,1,0:T(2,128)S(1)}, u32[]{:S(2)}, u32[]{:S(2)}) async-start(f32[16,2,512]{2,1,0:T(2,128)} %gather.1), calls=%async_computation.1 | async-start | bytes 131072 | tf_op jit(solution)/shard_map/all_to_all | solution.py:319

commit v4 on v3

--- a/solution.py
+++ b/solution.py
@@ -29,11 +29,10 @@
     return me >> 7, (me >> 5) & 3, (me >> 3) & 3, (me >> 1) & 3, me & 1
 
 
-def masked(rows, pattern_row, first):
+def masked(rows, hits):
     parts = []
     for b in range(rows.shape[0] // BLOCK):
-        hit = jnp.max(jnp.where(pattern_row == first + b, 1.0, 0.0).astype(F32), axis=1, keepdims=True)
-        parts.append(rows[b * BLOCK : (b + 1) * BLOCK, :] * hit.astype(BF16))
+        parts.append(rows[b * BLOCK : (b + 1) * BLOCK, :] * hits[b : b + 1, :].astype(BF16))
     return jnp.concatenate(parts, axis=0)
 
 
@@ -42,7 +41,7 @@
 
 
 STEP = 512
-LIMIT = 50
+LIMIT = 48
 ROUTES = (
     (1, 4, 2, 3, 7, 6, 5, 0),
     (4, 3, 2, 1, 0, 5, 7, 6),
@@ -63,99 +62,120 @@
     )
 
 
-def products(me, ancestor, panel, pattern):
+def hits_of(pattern_row, first, blocks):
+    ids = first + lax.broadcasted_iota(jnp.int32, (blocks, 1), 0)
+    return jnp.max(jnp.where(ids == pattern_row, 1.0, 0.0).astype(F32), axis=1, keepdims=True)
+
+
+def product_sent(me, ancestor, panel, pattern):
     height, breadth = ancestor.shape
     wide = panel.shape[2]
     steps = breadth // STEP
-
-    def kernel(me_ref, a_hbm, l_hbm, p_hbm, o_ref, k_ref, p_ref, a_buf, l_buf, acc, a_sem, l_sem, p_sem):
+    part = height // 4
+    each = STEP // BLOCK
+
+    def kernel(me_ref, a_hbm, l_hbm, p_hbm, o_ref, a_ref, f_ref, p_ref, l_buf, acc, a_sem, l_sem, f_sem, p_sem):
         zh, x, y, zl, c = place_of(me_ref[0])
+        s = 1 - c
         listed = pltpu.make_async_copy(p_hbm, p_ref, p_sem)
         listed.start()
-        order = (1 - c, c)
-        a_copies, l_copies = [], []
+        copies = []
         for k in range(steps):
             cols = pl.ds(k * STEP, STEP)
-            a_copies.append(pltpu.make_async_copy(a_hbm.at[:, cols], a_buf.at[k], a_sem.at[k]))
-            l_copies.append(
-                [
-                    pltpu.make_async_copy(l_hbm.at[order[i], cols, :], l_buf.at[i, k], l_sem.at[i, k])
-                    for i in range(2)
-                ]
+            copies.append(
+                (
+                    pltpu.make_async_copy(a_hbm.at[:, cols], a_ref.at[:, cols], a_sem.at[k]),
+                    pltpu.make_async_copy(l_hbm.at[s, cols, :], l_buf.at[k], l_sem.at[k]),
+                )
             )
-            a_copies[k].start()
-            l_copies[k][0].start()
-            l_copies[k][1].start()
-        listed.wait()
-        first = (zl * 2 + c) * (breadth // BLOCK)
-        for k in range(steps):
-            a_copies[k].wait()
-            for i in range(2):
-                l_copies[k][i].wait()
-                row = p_ref[pl.ds(order[i], 1), :]
-                rows = masked(l_buf[i, k], row, first + k * (STEP // BLOCK))
-                term = jnp.dot(a_buf[k], rows, preferred_element_type=F32)
-                total = acc if i == 0 else k_ref
-                if k == 0:
-                    total[...] = term
-                elif k == steps - 1 and i == 0:
-                    o_ref[...] = (total[...] + term).astype(BF16)
-                else:
-                    total[...] += term
-
-    return pl.pallas_call(
-        kernel,
-        in_specs=[scalars(), hbm(), hbm(), hbm()],
-        out_specs=[whole(), whole()],
-        out_shape=[
-            jax.ShapeDtypeStruct((height, wide), BF16),
-            jax.ShapeDtypeStruct((height, wide), F32),
-        ],
-        scratch_shapes=[
-            pltpu.VMEM(pattern.shape, pattern.dtype),
-            pltpu.VMEM((steps, height, STEP), BF16),
-            pltpu.VMEM((2, steps, STEP, wide), BF16),
-            pltpu.VMEM((height, wide), F32),
-            pltpu.SemaphoreType.DMA((steps,)),
-            pltpu.SemaphoreType.DMA((2, steps)),
-            pltpu.SemaphoreType.DMA,
-        ],
-        compiler_params=params(LIMIT),
-        cost_estimate=cost(height, breadth, 2 * wide),
-        name="products",
-    )(me, ancestor, panel, pattern)
-
-
-def pick(me, height, panel):
-    part, wide = height // 4, panel.shape[2]
-
-    def kernel(me_ref, l_hbm, f_ref, sem):
-        zh, x, y, zl, c = place_of(me_ref[0])
+            for copy in copies[k]:
+                copy.start()
         code = jnp.int32(0)
         for p, row in enumerate(ROUTES):
             code = jnp.where(zl * 2 + c == p, sum(v << (3 * q) for q, v in enumerate(row)), code)
         to = (code >> (3 * (zh * 4 + x))) & 7
-        copies = []
+        fetches = []
         for m in range(2):
             start = pl.multiple_of(y * height + ((to >> 1) ^ (2 * m)) * part, 16)
-            copies.append(
+            fetches.append(
                 pltpu.make_async_copy(
-                    l_hbm.at[to & 1, pl.ds(start, part), :], f_ref.at[pl.ds(m * part, part), :], sem.at[m]
+                    l_hbm.at[to & 1, pl.ds(start, part), :], f_ref.at[pl.ds(m * part, part), :], f_sem.at[m]
                 )
             )
-            copies[m].start()
-        for copy in copies:
+            fetches[m].start()
+        listed.wait()
+        hits = hits_of(p_ref[pl.ds(s, 1), :], (zl * 2 + c) * (breadth // BLOCK), breadth // BLOCK)
+        for k in range(steps):
+            for copy in copies[k]:
+                copy.wait()
+            rows = masked(l_buf[k], hits[k * each : (k + 1) * each, :])
+            term = jnp.dot(a_ref[:, k * STEP : (k + 1) * STEP], rows, preferred_element_type=F32)
+            if k == 0:
+                acc[...] = term
+            elif k < steps - 1:
+                acc[...] += term
+            else:
+                o_ref[...] = (acc[...] + term).astype(BF16)
+        for copy in fetches:
             copy.wait()
 
     return pl.pallas_call(
         kernel,
-        in_specs=[scalars(), hbm()],
-        out_specs=hbm(),
-        out_shape=jax.ShapeDtypeStruct((2 * part, wide), panel.dtype),
-        scratch_shapes=[pltpu.SemaphoreType.DMA((2,))],
+        in_specs=[scalars(), hbm(), hbm(), hbm()],
+        out_specs=[whole(), whole(), whole()],
+        out_shape=[
+            jax.ShapeDtypeStruct((height, wide), BF16),
+            jax.ShapeDtypeStruct((height, breadth), BF16),
+            jax.ShapeDtypeStruct((2 * part, wide), BF16),
+        ],
+        scratch_shapes=[
+            pltpu.VMEM(pattern.shape, pattern.dtype),
+            pltpu.VMEM((steps, STEP, wide), BF16),
+            pltpu.VMEM((height, wide), F32),
+            pltpu.SemaphoreType.DMA((steps,)),
+            pltpu.SemaphoreType.DMA((steps,)),
+            pltpu.SemaphoreType.DMA((2,)),
+            pltpu.SemaphoreType.DMA,
+        ],
         compiler_params=params(LIMIT),
-        name="pick",
-    )(me, panel)
+        cost_estimate=cost(height, breadth, wide),
+        name="product_sent",
+    )(me, ancestor, panel, pattern)
+
+
+def product_kept(me, ancestor, panel, pattern):
+    height, breadth = ancestor.shape
+    wide = panel.shape[2]
+    steps = breadth // STEP
+    each = STEP // BLOCK
+
+    def kernel(me_ref, a_ref, l_hbm, p_ref, o_ref, l_buf, l_sem):
+        zh, x, y, zl, s = place_of(me_ref[0])
+        copies = []
+        for k in range(steps):
+            rows = pl.ds(k * STEP, STEP)
+            copies.append(pltpu.make_async_copy(l_hbm.at[s, rows, :], l_buf.at[k], l_sem.at[k]))
+            copies[k].start()
+        hits = hits_of(p_ref[pl.ds(s, 1), :], (zl * 2 + s) * (breadth // BLOCK), breadth // BLOCK)
+        for k in range(steps):
+            copies[k].wait()
+            rows = masked(l_buf[k], hits[k * each : (k + 1) * each, :])
+            term = jnp.dot(a_ref[:, k * STEP : (k + 1) * STEP], rows, preferred_element_type=F32)
+            if k == 0:
+                o_ref[...] = term
+            else:
+                o_ref[...] += term
+
+    return pl.pallas_call(
+        kernel,
+        in_specs=[scalars(), whole(), hbm(), whole()],
+        out_specs=whole(),
+        out_shape=jax.ShapeDtypeStruct((height, wide), F32),
+        scratch_shapes=[pltpu.VMEM((steps, STEP, wide), BF16), pltpu.SemaphoreType.DMA((steps,))],
+        compiler_params=params(LIMIT),
+        cost_estimate=cost(height, breadth, wide),
+        name="product_kept",
+    )(me, ancestor, panel, pattern)
 
 
 def join(me, own, arrived):
@@ -230,11 +250,11 @@
     )(me, pattern, mine, near, far, arrived)
 
 
-def negate(me, height, pattern, half, arrived):
+def negate(me, height, pattern, half, arrived, after):
     part, wide = half.shape
     each = part // 2
 
-    def kernel(me_ref, p_ref, half_ref, in_ref, own_ref, send_ref, off):
+    def kernel(me_ref, p_ref, half_ref, in_ref, after_ref, own_ref, send_ref, off):
         zh, x, y, zl, core = place_of(me_ref[0])
         hit = chosen(((zh * 4 + x) * 4 + y) * height + zl * part, part, p_ref[pl.ds(core, 1), :])
         off[...] = -((half_ref[...] + in_ref[...].astype(F32)) * hit)
@@ -244,13 +264,13 @@
     piece = jax.ShapeDtypeStruct((each, wide), BF16)
     return pl.pallas_call(
         kernel,
-        in_specs=[scalars()] + [whole()] * 3,
+        in_specs=[scalars()] + [whole()] * 3 + [pl.BlockSpec(memory_space=pl.ANY)],
         out_specs=[whole()] * 2,
         out_shape=[piece, piece],
         scratch_shapes=[pltpu.VMEM((part, wide), F32)],
         compiler_params=params(),
         name="negate",
-    )(me, pattern, half, arrived)
+    )(me, pattern, half, arrived, after)
 
 
 def gather(pieces):
@@ -305,18 +325,20 @@
         me = jnp.reshape(lax.axis_index(every), (1,))
         core = lax.axis_index("c")
         height = ancestor.shape[0]
-        mine = lax.ppermute(pick(me, height, panel), every, fetch)
-        other, own = products(me, ancestor, panel, pattern)
+        other, held, picked = product_sent(me, ancestor, panel, pattern)
         swapped = lax.ppermute(other, "c", swap)
+        mine = lax.ppermute(picked, every, fetch)
+        own = product_kept(me, held, panel, pattern)
         near, far, sent = join(me, own, swapped)
         arrived = lax.ppermute(sent, "zl", xor4[1])
         half, sent, g = contract(me, height, pattern, mine, near, far, arrived)
         arrived = lax.ppermute(sent, "zl", xor4[2])
         pieces = lax.all_to_all(g, ("x", "y"), 0, 0, tiled=True)
-        off_own, off_send = negate(me, height, pattern, half, arrived)
+        gathered = gather(pieces)
+        off_own, off_send = negate(me, height, pattern, half, arrived, gathered)
         off_other = lax.ppermute(off_send, "c", swap)
         off = jnp.where(core == 0, jnp.stack([off_own, off_other]), jnp.stack([off_other, off_own]))
-        pieces = lax.all_to_all(gather(pieces), ("zh", "zl", "c"), 0, 0, tiled=True)
+        pieces = lax.all_to_all(gathered, ("zh", "zl", "c"), 0, 0, tiled=True)
         return off, finish(pieces, diag)
 
     rows = ("zh", "x", "y")

time: 66.5 us -> 61.6 us (0.926)
  Pallas kernels: 11.8 us -> 9.53 us
  starting transfers between devices: 26.4 us -> 25 us
  waiting for transfers between devices: 25.9 us -> 24.7 us
    ppermute x1, waiting for transfers between devices: 7.45 us -> 0.01 us  [local(): arrived = lax.ppermute(sent, 'zl', xor4[2])]
    all_to_all x1, waiting for transfers between devices: 0.01 us -> 6.56 us  [local(): pieces = lax.all_to_all(g, ('x', 'y'), 0, 0, tiled=True)]
    ppermute x1, waiting for transfers between devices: 4.11 us -> 0.01 us  [local(): mine = lax.ppermute(picked, every, fetch)]
    ppermute x1, waiting for transfers between devices: 7.24 us -> 11 us  [local(): arrived = lax.ppermute(sent, 'zl', xor4[1])]
    ppermute x1, starting transfers between devices: 6.02 us -> 2.41 us  [local(): arrived = lax.ppermute(sent, 'zl', xor4[2])]
    ppermute x1, starting transfers between devices: 0.58 us -> 3.56 us  [local(): off_other = lax.ppermute(off_send, 'c', swap)]
    all_to_all x1, starting transfers between devices: 6.46 us -> 4.01 us  [local(): pieces = lax.all_to_all(gathered, ('zh', 'zl', 'c'), 0, 0, tiled=True)]
    pallas_call x3, Pallas kernels: 9.06 us -> 6.76 us  [the longest x1 3.46 us: product_sent(): pl.pallas_call(kernel, in_specs=[scalars(), hbm(), hbm(), hbm()], out_spe...]
  transfers between devices with their start and end apart: 7 -> 7, of which waited for: 4 -> 3; matrix products, arithmetic and copies ran while one was open for 1% -> 1% of each run, Pallas kernels for 3% -> 6%
where the time goes in v4:
time: 61.6 us; the launch traced here: 61.3 us
  starting transfers between devices  25 us (41%)
  waiting for transfers between devices  24.7 us (40%)
  Pallas kernels  9.53 us (15%)
  between operations  0.72 us (1%)
  local copies, waits for them, and re-layouts  0.69 us (1%)
  other arithmetic  0.69 us (1%)
    ppermute x1, waiting for transfers between devices, local(): arrived = lax.ppermute(sent, 'zl', xor4[1])  11 us
    all_to_all x1, starting transfers between devices, local(): pieces = lax.all_to_all(g, ('x', 'y'), 0, 0, tiled=True)  7.87 us
    all_to_all x1, waiting for transfers between devices, local(): pieces = lax.all_to_all(gathered, ('zh', 'zl', 'c'), 0, 0, tiled=True)  7.12 us
    all_to_all x1, waiting for transfers between devices, local(): pieces = lax.all_to_all(g, ('x', 'y'), 0, 0, tiled=True)  6.56 us
    all_to_all x1, starting transfers between devices, local(): pieces = lax.all_to_all(gathered, ('zh', 'zl', 'c'), 0, 0, tiled=True)  4.01 us
    ppermute x1, starting transfers between devices, local(): off_other = lax.ppermute(off_send, 'c', swap)  3.56 us
    pallas_call x1, Pallas kernels, product_sent(): pl.pallas_call(kernel, in_specs=[scalars(), hbm(), hbm(), hbm()], out_spe...  3.46 us
    ppermute x1, starting transfers between devices, local(): swapped = lax.ppermute(other, 'c', swap)  3.39 us
  transfers between devices with their start and end apart: 7, of which 3 were waited for; matrix products, arithmetic and copies ran while one was open for 1% of the time, Pallas kernels for 6%

profile of v4, /device:TPU:1, one launch (start us, length us, event | category | flops | bytes accessed | tf_op | source)
XLA Modules:
  0.0 61.3 jit_solution(6530203639342322909)
XLA Ops:
  0.6 0.0 copy-start
  0.7 0.7 %copy-done = s32[2,80]{1,0:T(2,128)S(1)} copy-done((s32[2,80]{1,0:T(2,128)S(1)}, s32[2,80]{1,0:T(2,128)}, u32[]{:S(2)}) %copy-start) | copy-done | bytes 664
  1.3 3.5 %product_sent.1 = (bf16[640,512]{1,0:T(8,128)(2,1)S(1)}, bf16[640,2560]{1,0:T(8,128)(2,1)S(1)}, bf16[320,512]{1,0:T(8,128)(2,1)S(1)}) custom-call(s32[1]{0:T(128)} %bitcast.me_ref, bf16[640,2560]{1,0:T(8,128)(2,1)} %a_hbm.1, bf16[2,2560,512]{2,1,0:T(8,128)(2,1)} %l_hbm.3, s32[2,80]{1,0:T(2,128)S(1)} %copy-done), custom_call_target="tpu_custom_call" | custom-call | flops 1677721600 | bytes 6553600 | tf_op jit(solution)/shard_map/product_sent/pallas_call | solution.py:122
  4.8 3.4 %collective-permute-start.1 = (bf16[640,512]{1,0:T(8,128)(2,1)S(1)}, bf16[640,512]{1,0:T(8,128)(2,1)S(1)}, u32[]{:S(2)}, u32[]{:S(2)}) collective-permute-start(bf16[640,512]{1,0:T(8,128)(2,1)S(1)} %get-tuple-element.15), channel_id=1, source_target_pairs={{0,1},{1,0},{2,3},{3,2},{4,5},{5,4},{6,7},{7,6},{8,9},{9,8},{10,11... | collective-permute-start | bytes 1966088 | tf_op jit(solution)/shard_map/ppermute | solution.py:329
  8.2 2.1 %collective-permute-start = (bf16[320,512]{1,0:T(8,128)(2,1)S(1)}, bf16[320,512]{1,0:T(8,128)(2,1)S(1)}, u32[]{:S(2)}, u32[]{:S(2)}) collective-permute-start(bf16[320,512]{1,0:T(8,128)(2,1)S(1)} %get-tuple-element.13), channel_id=1, source_target_pairs={{0,1},{1,36},{2,67},{3,100},{4,129},{5,167},{6,192},{7,225},{8,9},... | collective-permute-start | bytes 983048 | tf_op jit(solution)/shard_map/ppermute | solution.py:330
  10.3 3.2 %product_kept.1.own_ref = f32[640,512]{1,0:T(8,128)S(1)} custom-call(s32[1]{0:T(128)} %bitcast.me_ref, bf16[640,2560]{1,0:T(8,128)(2,1)S(1)} %get-tuple-element.14.a_ref, bf16[2,2560,512]{2,1,0:T(8,128)(2,1)} %l_hbm.3, s32[2,80]{1,0:T(2,128)S(1)} %copy-done), custom_call_target="tpu_custom_call" | custom-call | flops 1677721600 | bytes 6553600 | tf_op jit(solution)/shard_map/product_kept/pallas_call | solution.py:169
  13.4 0.0 copy-start.1
  13.5 0.0 copy-start.2
  13.5 0.1 join.1
  13.6 1.7 %collective-permute-start.2 = (bf16[320,512]{1,0:T(8,128)(2,1)S(1)}, bf16[320,512]{1,0:T(8,128)(2,1)S(1)}, u32[]{:S(2)}, u32[]{:S(2)}) collective-permute-start(bf16[320,512]{1,0:T(8,128)(2,1)S(1)} %get-tuple-element.18), channel_id=1, source_target_pairs={{0,2},{2,0},{4,6},{6,4},{1,3},{3,1},{5,7},{7,5},{8,10},{10,8},{12,... | collective-permute-start | bytes 983048 | tf_op jit(solution)/shard_map/ppermute | solution.py:333
  15.3 0.0 collective-permute-done.m_ref
  15.3 11.0 %collective-permute-done.2.in_ref = bf16[320,512]{1,0:T(8,128)(2,1)S(1)} collective-permute-done((bf16[320,512]{1,0:T(8,128)(2,1)S(1)}, bf16[320,512]{1,0:T(8,128)(2,1)S(1)}, u32[]{:S(2)}, u32[]{:S(2)}) %collective-permute-start.2) | collective-permute-done | bytes 327712 | tf_op jit(solution)/shard_map/ppermute | solution.py:333
  26.3 1.4 %contract.1 = (f32[160,512]{1,0:T(8,128)S(1)}, bf16[160,512]{1,0:T(8,128)(2,1)S(1)}, bf16[16,32,512]{2,1,0:T(8,128)(2,1)}) custom-call(s32[1]{0:T(128)} %bitcast.me_ref, s32[2,80]{1,0:T(2,128)S(1)} %copy-done, bf16[320,512]{1,0:T(8,128)(2,1)S(1)} %collective-permute-done.m_ref, f32[160,512]{1,0:T(8,128)S(1)} %get-tuple-element.16.near_ref, ...), custom_call_target="tpu_custom_call" | custom-call | tf_op jit(solution)/shard_map/contract/pallas_call | solution.py:238
  27.6 7.9 %all-to-all-start = ((bf16[16,32,512]{2,1,0:T(8,128)(2,1)}), bf16[16,32,512]{2,1,0:T(8,128)(2,1)S(1)}, u32[]{:S(2)}, u32[]{:S(2)}) async-start(bf16[16,32,512]{2,1,0:T(8,128)(2,1)} %get-tuple-element.21), calls=%async_computation | async-start | bytes 1048576 | tf_op jit(solution)/shard_map/all_to_all | solution.py:336
  35.5 2.4 %collective-permute-start.3 = (bf16[160,512]{1,0:T(8,128)(2,1)S(1)}, bf16[160,512]{1,0:T(8,128)(2,1)S(1)}, u32[]{:S(2)}, u32[]{:S(2)}) collective-permute-start(bf16[160,512]{1,0:T(8,128)(2,1)S(1)} %get-tuple-element.20), channel_id=1, source_target_pairs={{0,4},{2,6},{4,0},{6,2},{1,5},{3,7},{5,1},{7,3},{8,12},{10,14},{12... | collective-permute-start | bytes 491528 | tf_op jit(solution)/shard_map/ppermute | solution.py:335
  37.9 6.6 %all-to-all-done.in_ref = bf16[16,32,512]{2,1,0:T(8,128)(2,1)S(1)} async-done(((bf16[16,32,512]{2,1,0:T(8,128)(2,1)}), bf16[16,32,512]{2,1,0:T(8,128)(2,1)S(1)}, u32[]{:S(2)}, u32[]{:S(2)}) %all-to-all-start) | async-done | bytes 524320 | tf_op jit(solution)/shard_map/all_to_all | solution.py:336
  44.5 0.7 %gather.1.after_ref = f32[16,2,512]{2,1,0:T(2,128)} custom-call(bf16[16,32,512]{2,1,0:T(8,128)(2,1)S(1)} %all-to-all-done.in_ref), custom_call_target="tpu_custom_call" | custom-call | tf_op jit(solution)/shard_map/gather/pallas_call | solution.py:286
  45.2 0.0 collective-permute-done.3.in_ref
  45.2 0.1 negate.1
  45.3 3.6 %collective-permute-start.4 = (bf16[80,512]{1,0:T(8,128)(2,1)S(1)}, bf16[80,512]{1,0:T(8,128)(2,1)S(1)}, u32[]{:S(2)}, u32[]{:S(2)}) collective-permute-start(bf16[80,512]{1,0:T(8,128)(2,1)S(1)} %get-tuple-element.23), channel_id=1, source_target_pairs={{0,1},{1,0},{2,3},{3,2},{4,5},{5,4},{6,7},{7,6},{8,9},{9,8},{10,11... | collective-permute-start | bytes 245768 | tf_op jit(solution)/shard_map/ppermute | solution.py:339
  48.9 4.0 %all-to-all-start.1 = ((f32[16,2,512]{2,1,0:T(2,128)}), f32[16,2,512]{2,1,0:T(2,128)S(1)}, u32[]{:S(2)}, u32[]{:S(2)}) async-start(f32[16,2,512]{2,1,0:T(2,128)} %gather.1.after_ref), calls=%async_computation.1 | async-start | bytes 131072 | tf_op jit(solution)/shard_map/all_to_all | solution.py:341
  52.9 0.7 %maximum_select_fusion = bf16[2,80,512]{2,1,0:T(8,128)(2,1)} fusion(bf16[1,80,512]{2,1,0:T(8,128)(2,1)S(1)} %bitcast.4, bf16[1,80,512]{2,1,0:T(8,128)(2,1)S(1)} %bitcast.3, pred[]{:T(512)S(6)} %eq.3), kind=kLoop, calls=%fused_computation | loop fusion | flops 245760 | bytes 327681 | tf_op jit(solution)/shard_map/jit(_where)/select_n | solution.py:340
  53.6 7.1 %all-to-all-done.1.in_ref = f32[16,2,512]{2,1,0:T(2,128)S(1)} async-done(((f32[16,2,512]{2,1,0:T(2,128)}), f32[16,2,512]{2,1,0:T(2,128)S(1)}, u32[]{:S(2)}, u32[]{:S(2)}) %all-to-all-start.1) | async-done | bytes 65568 | tf_op jit(solution)/shard_map/all_to_all | solution.py:341
  60.7 0.6 finish.1
  (4 shorter events, 0.0 us)
Async XLA Ops:
  0.6 0.7 %copy-start = (s32[2,80]{1,0:T(2,128)S(1)}, s32[2,80]{1,0:T(2,128)}, u32[]{:S(2)}) copy-start(s32[2,80]{1,0:T(2,128)} %p_ref.5) | copy-start | bytes 1924
  4.8 8.7 %collective-permute-start.1 = (bf16[640,512]{1,0:T(8,128)(2,1)S(1)}, bf16[640,512]{1,0:T(8,128)(2,1)S(1)}, u32[]{:S(2)}, u32[]{:S(2)}) collective-permute-start(bf16[640,512]{1,0:T(8,128)(2,1)S(1)} %get-tuple-element.15), channel_id=1, source_target_pairs={{0,1},{1,0},{2,3},{3,2},{4,5},{5,4},{6,7},{7,6},{8,9},{9,8},{10,11... | collective-permute-start | bytes 1966088 | tf_op jit(solution)/shard_map/ppermute | solution.py:329
  8.2 7.1 %collective-permute-start = (bf16[320,512]{1,0:T(8,128)(2,1)S(1)}, bf16[320,512]{1,0:T(8,128)(2,1)S(1)}, u32[]{:S(2)}, u32[]{:S(2)}) collective-permute-start(bf16[320,512]{1,0:T(8,128)(2,1)S(1)} %get-tuple-element.13), channel_id=1, source_target_pairs={{0,1},{1,36},{2,67},{3,100},{4,129},{5,167},{6,192},{7,225},{8,9},... | collective-permute-start | bytes 983048 | tf_op jit(solution)/shard_map/ppermute | solution.py:330
  13.4 31.7 %copy-start.1 = (s32[2,80]{1,0:T(2,128)S(1)}, s32[2,80]{1,0:T(2,128)}, u32[]{:S(2)}) copy-start(s32[2,80]{1,0:T(2,128)} %p_ref.5) | copy-start | bytes 1924
  13.5 47.2 %copy-start.2 = (f32[2,2,512]{2,1,0:T(2,128)S(1)}, f32[2,2,512]{2,1,0:T(2,128)}, u32[]{:S(2)}) copy-start(f32[2,2,512]{2,1,0:T(2,128)} %d_ref.1) | copy-start | bytes 24580
  13.6 12.7 %collective-permute-start.2 = (bf16[320,512]{1,0:T(8,128)(2,1)S(1)}, bf16[320,512]{1,0:T(8,128)(2,1)S(1)}, u32[]{:S(2)}, u32[]{:S(2)}) collective-permute-start(bf16[320,512]{1,0:T(8,128)(2,1)S(1)} %get-tuple-element.18), channel_id=1, source_target_pairs={{0,2},{2,0},{4,6},{6,4},{1,3},{3,1},{5,7},{7,5},{8,10},{10,8},{12,... | collective-permute-start | bytes 983048 | tf_op jit(solution)/shard_map/ppermute | solution.py:333
  27.6 16.8 %all-to-all-start = ((bf16[16,32,512]{2,1,0:T(8,128)(2,1)}), bf16[16,32,512]{2,1,0:T(8,128)(2,1)S(1)}, u32[]{:S(2)}, u32[]{:S(2)}) async-start(bf16[16,32,512]{2,1,0:T(8,128)(2,1)} %get-tuple-element.21), calls=%async_computation | async-start | bytes 1048576 | tf_op jit(solution)/shard_map/all_to_all | solution.py:336
  35.5 9.7 %collective-permute-start.3 = (bf16[160,512]{1,0:T(8,128)(2,1)S(1)}, bf16[160,512]{1,0:T(8,128)(2,1)S(1)}, u32[]{:S(2)}, u32[]{:S(2)}) collective-permute-start(bf16[160,512]{1,0:T(8,128)(2,1)S(1)} %get-tuple-element.20), channel_id=1, source_target_pairs={{0,4},{2,6},{4,0},{6,2},{1,5},{3,7},{5,1},{7,3},{8,12},{10,14},{12... | collective-permute-start | bytes 491528 | tf_op jit(solution)/shard_map/ppermute | solution.py:335
  45.3 7.6 %collective-permute-start.4 = (bf16[80,512]{1,0:T(8,128)(2,1)S(1)}, bf16[80,512]{1,0:T(8,128)(2,1)S(1)}, u32[]{:S(2)}, u32[]{:S(2)}) collective-permute-start(bf16[80,512]{1,0:T(8,128)(2,1)S(1)} %get-tuple-element.23), channel_id=1, source_target_pairs={{0,1},{1,0},{2,3},{3,2},{4,5},{5,4},{6,7},{7,6},{8,9},{9,8},{10,11... | collective-permute-start | bytes 245768 | tf_op jit(solution)/shard_map/ppermute | solution.py:339
  48.9 11.8 %all-to-all-start.1 = ((f32[16,2,512]{2,1,0:T(2,128)}), f32[16,2,512]{2,1,0:T(2,128)S(1)}, u32[]{:S(2)}, u32[]{:S(2)}) async-start(f32[16,2,512]{2,1,0:T(2,128)} %gather.1.after_ref), calls=%async_computation.1 | async-start | bytes 131072 | tf_op jit(solution)/shard_map/all_to_all | solution.py:341

commit v5 on v4

--- a/solution.py
+++ b/solution.py
@@ -143,13 +143,16 @@
     )(me, ancestor, panel, pattern)
 
 
-def product_kept(me, ancestor, panel, pattern):
+def product_rows(me, ancestor, panel, pattern, arrived, quarters):
     height, breadth = ancestor.shape
     wide = panel.shape[2]
     steps = breadth // STEP
     each = STEP // BLOCK
-
-    def kernel(me_ref, a_ref, l_hbm, p_ref, o_ref, l_buf, l_sem):
+    part = height // 4
+    sent = 0 not in quarters
+
+    def kernel(me_ref, a_ref, l_hbm, p_ref, in_ref, *rest):
+        outs, (l_buf, acc, l_sem) = rest[:-3], rest[-3:]
         zh, x, y, zl, s = place_of(me_ref[0])
         copies = []
         for k in range(steps):
@@ -157,52 +160,36 @@
             copies.append(pltpu.make_async_copy(l_hbm.at[s, rows, :], l_buf.at[k], l_sem.at[k]))
             copies[k].start()
         hits = hits_of(p_ref[pl.ds(s, 1), :], (zl * 2 + s) * (breadth // BLOCK), breadth // BLOCK)
+        places = [pl.ds(pl.multiple_of((zl ^ m) * part, 16), part) for m in quarters]
+        for i, at in enumerate(places):
+            acc[i * part : (i + 1) * part, :] = in_ref[at, :].astype(F32)
         for k in range(steps):
             copies[k].wait()
-            rows = masked(l_buf[k], hits[k * each : (k + 1) * each, :])
-            term = jnp.dot(a_ref[:, k * STEP : (k + 1) * STEP], rows, preferred_element_type=F32)
-            if k == 0:
-                o_ref[...] = term
-            else:
-                o_ref[...] += term
-
-    return pl.pallas_call(
-        kernel,
-        in_specs=[scalars(), whole(), hbm(), whole()],
-        out_specs=whole(),
-        out_shape=jax.ShapeDtypeStruct((height, wide), F32),
-        scratch_shapes=[pltpu.VMEM((steps, STEP, wide), BF16), pltpu.SemaphoreType.DMA((steps,))],
+            right = masked(l_buf[k], hits[k * each : (k + 1) * each, :])
+            left = jnp.concatenate([a_ref[at, k * STEP : (k + 1) * STEP] for at in places], axis=0)
+            acc[...] += jnp.dot(left, right, preferred_element_type=F32)
+        if sent:
+            outs[0][...] = acc[...].astype(BF16)
+        else:
+            for i, out in enumerate(outs):
+                out[...] = acc[i * part : (i + 1) * part, :]
+
+    piece = jax.ShapeDtypeStruct((part, wide), F32)
+    shapes = [jax.ShapeDtypeStruct((2 * part, wide), BF16)] if sent else [piece, piece]
+    return pl.pallas_call(
+        kernel,
+        in_specs=[scalars(), whole(), hbm(), whole(), whole()],
+        out_specs=[whole()] * len(shapes),
+        out_shape=shapes,
+        scratch_shapes=[
+            pltpu.VMEM((steps, STEP, wide), BF16),
+            pltpu.VMEM((2 * part, wide), F32),
+            pltpu.SemaphoreType.DMA((steps,)),
+        ],
         compiler_params=params(LIMIT),
-        cost_estimate=cost(height, breadth, wide),
-        name="product_kept",
-    )(me, ancestor, panel, pattern)
-
-
-def join(me, own, arrived):
-    height, wide = own.shape
-    part = height // 4
-
-    def kernel(me_ref, own_ref, in_ref, near_ref, far_ref, sent_ref):
-        here = place_of(me_ref[0])[3]
-        for m in range(4):
-            rows = pl.ds(pl.multiple_of((here ^ m) * part, 16), part)
-            total = own_ref[rows, :] + in_ref[rows, :].astype(F32)
-            if m == 0:
-                near_ref[...] = total
-            elif m == 2:
-                far_ref[...] = total
-            else:
-                sent_ref[(m // 2) * part : (m // 2 + 1) * part, :] = total.astype(BF16)
-
-    piece = jax.ShapeDtypeStruct((part, wide), F32)
-    return pl.pallas_call(
-        kernel,
-        in_specs=[scalars(), whole(), whole()],
-        out_specs=[whole()] * 3,
-        out_shape=[piece, piece, jax.ShapeDtypeStruct((2 * part, wide), BF16)],
-        compiler_params=params(),
-        name="join",
-    )(me, own, arrived)
+        cost_estimate=cost(height // 2, breadth, wide),
+        name="product_rows",
+    )(me, ancestor, panel, pattern, arrived)
 
 
 def chosen(first, count, pattern_row):
@@ -328,9 +315,9 @@
         other, held, picked = product_sent(me, ancestor, panel, pattern)
         swapped = lax.ppermute(other, "c", swap)
         mine = lax.ppermute(picked, every, fetch)
-        own = product_kept(me, held, panel, pattern)
-        near, far, sent = join(me, own, swapped)
+        (sent,) = product_rows(me, held, panel, pattern, swapped, (1, 3))
         arrived = lax.ppermute(sent, "zl", xor4[1])
+        near, far = product_rows(me, held, panel, pattern, swapped, (0, 2))
         half, sent, g = contract(me, height, pattern, mine, near, far, arrived)
         arrived = lax.ppermute(sent, "zl", xor4[2])
         pieces = lax.all_to_all(g, ("x", "y"), 0, 0, tiled=True)

time: 61.6 us -> 60.9 us (0.989)
  starting transfers between devices: 25 us -> 23.6 us
  Pallas kernels: 9.53 us -> 10.9 us
  waiting for transfers between devices: 24.7 us -> 24 us
    ppermute x1, waiting for transfers between devices: 11 us -> 9.15 us  [local(): arrived = lax.ppermute(sent, 'zl', xor4[1])]
    pallas_call x2, Pallas kernels: 3.28 us -> 4.65 us  [product_rows(): pl.pallas_call(kernel, in_specs=[scalars(), whole(), hbm(), whole(), whol...]
    all_to_all x1, waiting for transfers between devices: 6.56 us -> 7.68 us  [local(): pieces = lax.all_to_all(g, ('x', 'y'), 0, 0, tiled=True)]
    ppermute x1, starting transfers between devices: 3.56 us -> 2.68 us  [local(): off_other = lax.ppermute(off_send, 'c', swap)]
  transfers between devices with their start and end apart: 7 -> 7, of which waited for: 3 -> 3; matrix products, arithmetic and copies ran while one was open for 1% -> 1% of each run, Pallas kernels for 6% -> 9%
where the time goes in v5:
time: 60.9 us; the launch traced here: 60.5 us
  waiting for transfers between devices  24 us (39%)
  starting transfers between devices  23.6 us (39%)
  Pallas kernels  10.9 us (18%)
  between operations  0.72 us (1%)
  local copies, waits for them, and re-layouts  0.69 us (1%)
  other arithmetic  0.69 us (1%)
    ppermute x1, waiting for transfers between devices, local(): arrived = lax.ppermute(sent, 'zl', xor4[1])  9.15 us
    all_to_all x1, starting transfers between devices, local(): pieces = lax.all_to_all(g, ('x', 'y'), 0, 0, tiled=True)  7.84 us
    all_to_all x1, waiting for transfers between devices, local(): pieces = lax.all_to_all(g, ('x', 'y'), 0, 0, tiled=True)  7.68 us
    all_to_all x1, waiting for transfers between devices, local(): pieces = lax.all_to_all(gathered, ('zh', 'zl', 'c'), 0, 0, tiled=True)  7.12 us
    pallas_call x2, Pallas kernels, product_rows(): pl.pallas_call(kernel, in_specs=[scalars(), whole(), hbm(), whole(), whol...  4.65 us
    all_to_all x1, starting transfers between devices, local(): pieces = lax.all_to_all(gathered, ('zh', 'zl', 'c'), 0, 0, tiled=True)  3.77 us
    pallas_call x1, Pallas kernels, product_sent(): pl.pallas_call(kernel, in_specs=[scalars(), hbm(), hbm(), hbm()], out_spe...  3.46 us
    ppermute x1, starting transfers between devices, local(): swapped = lax.ppermute(other, 'c', swap)  3.39 us
  transfers between devices with their start and end apart: 7, of which 3 were waited for; matrix products, arithmetic and copies ran while one was open for 1% of the time, Pallas kernels for 9%

profile of v5, /device:TPU:1, one launch (start us, length us, event | category | flops | bytes accessed | tf_op | source)
XLA Modules:
  0.0 60.5 jit_solution(17993193507390327747)
XLA Ops:
  0.6 0.0 copy-start
  0.7 0.7 %copy-done = s32[2,80]{1,0:T(2,128)S(1)} copy-done((s32[2,80]{1,0:T(2,128)S(1)}, s32[2,80]{1,0:T(2,128)}, u32[]{:S(2)}) %copy-start) | copy-done | bytes 664
  1.3 3.5 %product_sent.1 = (bf16[640,512]{1,0:T(8,128)(2,1)S(1)}, bf16[640,2560]{1,0:T(8,128)(2,1)S(1)}, bf16[320,512]{1,0:T(8,128)(2,1)S(1)}) custom-call(s32[1]{0:T(128)} %bitcast.me_ref, bf16[640,2560]{1,0:T(8,128)(2,1)} %a_hbm.1, bf16[2,2560,512]{2,1,0:T(8,128)(2,1)} %l_hbm.5, s32[2,80]{1,0:T(2,128)S(1)} %copy-done), custom_call_target="tpu_custom_call" | custom-call | flops 1677721600 | bytes 6553600 | tf_op jit(solution)/shard_map/product_sent/pallas_call | solution.py:122
  4.8 3.4 %collective-permute-start.1 = (bf16[640,512]{1,0:T(8,128)(2,1)S(1)}, bf16[640,512]{1,0:T(8,128)(2,1)S(1)}, u32[]{:S(2)}, u32[]{:S(2)}) collective-permute-start(bf16[640,512]{1,0:T(8,128)(2,1)S(1)} %get-tuple-element.14), channel_id=1, source_target_pairs={{0,1},{1,0},{2,3},{3,2},{4,5},{5,4},{6,7},{7,6},{8,9},{9,8},{10,11... | collective-permute-start | bytes 1966088 | tf_op jit(solution)/shard_map/ppermute | solution.py:316
  8.2 2.1 %collective-permute-start = (bf16[320,512]{1,0:T(8,128)(2,1)S(1)}, bf16[320,512]{1,0:T(8,128)(2,1)S(1)}, u32[]{:S(2)}, u32[]{:S(2)}) collective-permute-start(bf16[320,512]{1,0:T(8,128)(2,1)S(1)} %get-tuple-element.12), channel_id=1, source_target_pairs={{0,1},{1,36},{2,67},{3,100},{4,129},{5,167},{6,192},{7,225},{8,9},... | collective-permute-start | bytes 983048 | tf_op jit(solution)/shard_map/ppermute | solution.py:317
  10.3 0.0 collective-permute-done.1.in_ref
  10.3 2.3 %product_rows.3 = bf16[320,512]{1,0:T(8,128)(2,1)S(1)} custom-call(s32[1]{0:T(128)} %bitcast.me_ref, bf16[640,2560]{1,0:T(8,128)(2,1)S(1)} %get-tuple-element.13.a_ref, bf16[2,2560,512]{2,1,0:T(8,128)(2,1)} %l_hbm.5, s32[2,80]{1,0:T(2,128)S(1)} %copy-done, bf16[640,512]{1,0:T(8,128)(2,1)S(1)} %collective-permute-done.1.in_ref), custom_call_target="tpu_custom_call" | custom-call | flops 838860800 | bytes 4587520 | tf_op jit(solution)/shard_map/product_rows/pallas_call | solution.py:179
  12.6 0.0 copy-start.1
  12.6 1.6 %collective-permute-start.2 = (bf16[320,512]{1,0:T(8,128)(2,1)S(1)}, bf16[320,512]{1,0:T(8,128)(2,1)S(1)}, u32[]{:S(2)}, u32[]{:S(2)}) collective-permute-start(bf16[320,512]{1,0:T(8,128)(2,1)S(1)} %product_rows.3), channel_id=1, source_target_pairs={{0,2},{2,0},{4,6},{6,4},{1,3},{3,1},{5,7},{7,5},{8,10},{10,8},{12,... | collective-permute-start | bytes 983048 | tf_op jit(solution)/shard_map/ppermute | solution.py:319
  14.3 2.3 %product_rows.2 = (f32[160,512]{1,0:T(8,128)S(1)}, f32[160,512]{1,0:T(8,128)S(1)}) custom-call(s32[1]{0:T(128)} %bitcast.me_ref, bf16[640,2560]{1,0:T(8,128)(2,1)S(1)} %get-tuple-element.13.a_ref, bf16[2,2560,512]{2,1,0:T(8,128)(2,1)} %l_hbm.5, s32[2,80]{1,0:T(2,128)S(1)} %copy-done, bf16[640,512]{1,0:T(8,128)(2,1)S(1)} %collective-permute-done.1.in_ref), custom_call_target="tpu_custom_call" | custom-call | flops 838860800 | bytes 4587520 | tf_op jit(solution)/shard_map/product_rows/pallas_call | solution.py:179
  16.6 0.0 copy-start.2
  16.6 0.0 collective-permute-done.m_ref
  16.6 9.2 %collective-permute-done.2.in_ref = bf16[320,512]{1,0:T(8,128)(2,1)S(1)} collective-permute-done((bf16[320,512]{1,0:T(8,128)(2,1)S(1)}, bf16[320,512]{1,0:T(8,128)(2,1)S(1)}, u32[]{:S(2)}, u32[]{:S(2)}) %collective-permute-start.2) | collective-permute-done | bytes 327712 | tf_op jit(solution)/shard_map/ppermute | solution.py:319
  25.8 1.4 %contract.1 = (f32[160,512]{1,0:T(8,128)S(1)}, bf16[160,512]{1,0:T(8,128)(2,1)S(1)}, bf16[16,32,512]{2,1,0:T(8,128)(2,1)}) custom-call(s32[1]{0:T(128)} %bitcast.me_ref, s32[2,80]{1,0:T(2,128)S(1)} %copy-done, bf16[320,512]{1,0:T(8,128)(2,1)S(1)} %collective-permute-done.m_ref, f32[160,512]{1,0:T(8,128)S(1)} %get-tuple-element.15.near_ref, ...), custom_call_target="tpu_custom_call" | custom-call | tf_op jit(solution)/shard_map/contract/pallas_call | solution.py:225
  27.1 7.8 %all-to-all-start = ((bf16[16,32,512]{2,1,0:T(8,128)(2,1)}), bf16[16,32,512]{2,1,0:T(8,128)(2,1)S(1)}, u32[]{:S(2)}, u32[]{:S(2)}) async-start(bf16[16,32,512]{2,1,0:T(8,128)(2,1)} %get-tuple-element.19), calls=%async_computation | async-start | bytes 1048576 | tf_op jit(solution)/shard_map/all_to_all | solution.py:323
  35.0 2.2 %collective-permute-start.3 = (bf16[160,512]{1,0:T(8,128)(2,1)S(1)}, bf16[160,512]{1,0:T(8,128)(2,1)S(1)}, u32[]{:S(2)}, u32[]{:S(2)}) collective-permute-start(bf16[160,512]{1,0:T(8,128)(2,1)S(1)} %get-tuple-element.18), channel_id=1, source_target_pairs={{0,4},{2,6},{4,0},{6,2},{1,5},{3,7},{5,1},{7,3},{8,12},{10,14},{12... | collective-permute-start | bytes 491528 | tf_op jit(solution)/shard_map/ppermute | solution.py:322
  37.2 7.7 %all-to-all-done.in_ref = bf16[16,32,512]{2,1,0:T(8,128)(2,1)S(1)} async-done(((bf16[16,32,512]{2,1,0:T(8,128)(2,1)}), bf16[16,32,512]{2,1,0:T(8,128)(2,1)S(1)}, u32[]{:S(2)}, u32[]{:S(2)}) %all-to-all-start) | async-done | bytes 524320 | tf_op jit(solution)/shard_map/all_to_all | solution.py:323
  44.8 0.7 %gather.1.after_ref = f32[16,2,512]{2,1,0:T(2,128)} custom-call(bf16[16,32,512]{2,1,0:T(8,128)(2,1)S(1)} %all-to-all-done.in_ref), custom_call_target="tpu_custom_call" | custom-call | tf_op jit(solution)/shard_map/gather/pallas_call | solution.py:273
  45.5 0.1 negate.1
  45.7 2.7 %collective-permute-start.4 = (bf16[80,512]{1,0:T(8,128)(2,1)S(1)}, bf16[80,512]{1,0:T(8,128)(2,1)S(1)}, u32[]{:S(2)}, u32[]{:S(2)}) collective-permute-start(bf16[80,512]{1,0:T(8,128)(2,1)S(1)} %get-tuple-element.21), channel_id=1, source_target_pairs={{0,1},{1,0},{2,3},{3,2},{4,5},{5,4},{6,7},{7,6},{8,9},{9,8},{10,11... | collective-permute-start | bytes 245768 | tf_op jit(solution)/shard_map/ppermute | solution.py:326
  48.4 3.8 %all-to-all-start.1 = ((f32[16,2,512]{2,1,0:T(2,128)}), f32[16,2,512]{2,1,0:T(2,128)S(1)}, u32[]{:S(2)}, u32[]{:S(2)}) async-start(f32[16,2,512]{2,1,0:T(2,128)} %gather.1.after_ref), calls=%async_computation.1 | async-start | bytes 131072 | tf_op jit(solution)/shard_map/all_to_all | solution.py:328
  52.1 0.7 %maximum_select_fusion = bf16[2,80,512]{2,1,0:T(8,128)(2,1)} fusion(bf16[1,80,512]{2,1,0:T(8,128)(2,1)S(1)} %bitcast.4, bf16[1,80,512]{2,1,0:T(8,128)(2,1)S(1)} %bitcast.3, pred[]{:T(512)S(6)} %eq.3), kind=kLoop, calls=%fused_computation | loop fusion | flops 245760 | bytes 327681 | tf_op jit(solution)/shard_map/jit(_where)/select_n | solution.py:327
  52.8 7.1 %all-to-all-done.1.in_ref = f32[16,2,512]{2,1,0:T(2,128)S(1)} async-done(((f32[16,2,512]{2,1,0:T(2,128)}), f32[16,2,512]{2,1,0:T(2,128)S(1)}, u32[]{:S(2)}, u32[]{:S(2)}) %all-to-all-start.1) | async-done | bytes 65568 | tf_op jit(solution)/shard_map/all_to_all | solution.py:328
  59.9 0.6 %finish.1 = f32[2,2,512]{2,1,0:T(2,128)} custom-call(f32[16,2,512]{2,1,0:T(2,128)S(1)} %all-to-all-done.1.in_ref, f32[2,2,512]{2,1,0:T(2,128)S(1)} %copy-done.2), custom_call_target="tpu_custom_call" | custom-call | tf_op jit(solution)/shard_map/finish/pallas_call | solution.py:291
  (4 shorter events, 0.0 us)
Async XLA Ops:
  0.6 0.7 %copy-start = (s32[2,80]{1,0:T(2,128)S(1)}, s32[2,80]{1,0:T(2,128)}, u32[]{:S(2)}) copy-start(s32[2,80]{1,0:T(2,128)} %p_ref.7) | copy-start | bytes 1924
  4.8 5.5 %collective-permute-start.1 = (bf16[640,512]{1,0:T(8,128)(2,1)S(1)}, bf16[640,512]{1,0:T(8,128)(2,1)S(1)}, u32[]{:S(2)}, u32[]{:S(2)}) collective-permute-start(bf16[640,512]{1,0:T(8,128)(2,1)S(1)} %get-tuple-element.14), channel_id=1, source_target_pairs={{0,1},{1,0},{2,3},{3,2},{4,5},{5,4},{6,7},{7,6},{8,9},{9,8},{10,11... | collective-permute-start | bytes 1966088 | tf_op jit(solution)/shard_map/ppermute | solution.py:316
  8.2 8.4 %collective-permute-start = (bf16[320,512]{1,0:T(8,128)(2,1)S(1)}, bf16[320,512]{1,0:T(8,128)(2,1)S(1)}, u32[]{:S(2)}, u32[]{:S(2)}) collective-permute-start(bf16[320,512]{1,0:T(8,128)(2,1)S(1)} %get-tuple-element.12), channel_id=1, source_target_pairs={{0,1},{1,36},{2,67},{3,100},{4,129},{5,167},{6,192},{7,225},{8,9},... | collective-permute-start | bytes 983048 | tf_op jit(solution)/shard_map/ppermute | solution.py:317
  12.6 32.9 %copy-start.1 = (s32[2,80]{1,0:T(2,128)S(1)}, s32[2,80]{1,0:T(2,128)}, u32[]{:S(2)}) copy-start(s32[2,80]{1,0:T(2,128)} %p_ref.7) | copy-start | bytes 1924
  12.6 13.1 %collective-permute-start.2 = (bf16[320,512]{1,0:T(8,128)(2,1)S(1)}, bf16[320,512]{1,0:T(8,128)(2,1)S(1)}, u32[]{:S(2)}, u32[]{:S(2)}) collective-permute-start(bf16[320,512]{1,0:T(8,128)(2,1)S(1)} %product_rows.3), channel_id=1, source_target_pairs={{0,2},{2,0},{4,6},{6,4},{1,3},{3,1},{5,7},{7,5},{8,10},{10,8},{12,... | collective-permute-start | bytes 983048 | tf_op jit(solution)/shard_map/ppermute | solution.py:319
  16.6 43.3 %copy-start.2 = (f32[2,2,512]{2,1,0:T(2,128)S(1)}, f32[2,2,512]{2,1,0:T(2,128)}, u32[]{:S(2)}) copy-start(f32[2,2,512]{2,1,0:T(2,128)} %d_ref.1) | copy-start | bytes 24580
  27.1 17.7 %all-to-all-start = ((bf16[16,32,512]{2,1,0:T(8,128)(2,1)}), bf16[16,32,512]{2,1,0:T(8,128)(2,1)S(1)}, u32[]{:S(2)}, u32[]{:S(2)}) async-start(bf16[16,32,512]{2,1,0:T(8,128)(2,1)} %get-tuple-element.19), calls=%async_computation | async-start | bytes 1048576 | tf_op jit(solution)/shard_map/all_to_all | solution.py:323
  35.0 10.5 %collective-permute-start.3 = (bf16[160,512]{1,0:T(8,128)(2,1)S(1)}, bf16[160,512]{1,0:T(8,128)(2,1)S(1)}, u32[]{:S(2)}, u32[]{:S(2)}) collective-permute-start(bf16[160,512]{1,0:T(8,128)(2,1)S(1)} %get-tuple-element.18), channel_id=1, source_target_pairs={{0,4},{2,6},{4,0},{6,2},{1,5},{3,7},{5,1},{7,3},{8,12},{10,14},{12... | collective-permute-start | bytes 491528 | tf_op jit(solution)/shard_map/ppermute | solution.py:322
  45.7 6.5 %collective-permute-start.4 = (bf16[80,512]{1,0:T(8,128)(2,1)S(1)}, bf16[80,512]{1,0:T(8,128)(2,1)S(1)}, u32[]{:S(2)}, u32[]{:S(2)}) collective-permute-start(bf16[80,512]{1,0:T(8,128)(2,1)S(1)} %get-tuple-element.21), channel_id=1, source_target_pairs={{0,1},{1,0},{2,3},{3,2},{4,5},{5,4},{6,7},{7,6},{8,9},{9,8},{10,11... | collective-permute-start | bytes 245768 | tf_op jit(solution)/shard_map/ppermute | solution.py:326
  48.4 11.6 %all-to-all-start.1 = ((f32[16,2,512]{2,1,0:T(2,128)}), f32[16,2,512]{2,1,0:T(2,128)S(1)}, u32[]{:S(2)}, u32[]{:S(2)}) async-start(f32[16,2,512]{2,1,0:T(2,128)} %gather.1.after_ref), calls=%async_computation.1 | async-start | bytes 131072 | tf_op jit(solution)/shard_map/all_to_all | solution.py:328

commit v6 on v5

--- a/solution.py
+++ b/solution.py
@@ -260,6 +260,23 @@
     )(me, pattern, half, arrived, after)
 
 
+def assemble(me, own, other):
+    def kernel(me_ref, own_ref, other_ref, o_ref):
+        core = me_ref[0] & 1
+        o_ref[core] = own_ref[...]
+        o_ref[1 - core] = other_ref[...]
+
+    return pl.pallas_call(
+        kernel,
+        in_specs=[scalars(), whole(), whole()],
+        out_specs=whole(),
+        out_shape=jax.ShapeDtypeStruct((2, *own.shape), own.dtype),
+        compiler_params=params(),
+        cost_estimate=pl.CostEstimate(flops=1, bytes_accessed=1, transcendentals=0),
+        name="assemble",
+    )(me, own, other)
+
+
 def gather(pieces):
     count, tall, wide = pieces.shape
 
@@ -310,7 +327,6 @@
 
     def local(ancestor, panel, pattern, diag):
         me = jnp.reshape(lax.axis_index(every), (1,))
-        core = lax.axis_index("c")
         height = ancestor.shape[0]
         other, held, picked = product_sent(me, ancestor, panel, pattern)
         swapped = lax.ppermute(other, "c", swap)
@@ -324,7 +340,7 @@
         gathered = gather(pieces)
         off_own, off_send = negate(me, height, pattern, half, arrived, gathered)
         off_other = lax.ppermute(off_send, "c", swap)
-        off = jnp.where(core == 0, jnp.stack([off_own, off_other]), jnp.stack([off_other, off_own]))
+        off = assemble(me, off_own, off_other)
         pieces = lax.all_to_all(gathered, ("zh", "zl", "c"), 0, 0, tiled=True)
         return off, finish(pieces, diag)
 

time: 60.9 us -> 60.5 us (level)
  waiting for transfers between devices: 24 us -> 22.8 us
  starting transfers between devices: 23.6 us -> 24.4 us
  Pallas kernels: 10.9 us -> 11.6 us
  other arithmetic: 0.69 us -> 0 us
    all_to_all x1, starting transfers between devices: 3.77 us -> 7.09 us  [local(): pieces = lax.all_to_all(gathered, ('zh', 'zl', 'c'), 0, 0, tiled=True)]
    ppermute x1, starting transfers between devices: 2.68 us -> 0.19 us  [local(): off_other = lax.ppermute(off_send, 'c', swap)]
    all_to_all x1, waiting for transfers between devices: 7.12 us -> 5.6 us  [local(): pieces = lax.all_to_all(gathered, ('zh', 'zl', 'c'), 0, 0, tiled=True)]
    ppermute x1, waiting for transfers between devices: 0.01 us -> 1.17 us  [local(): off_other = lax.ppermute(off_send, 'c', swap)]
    all_to_all x1, waiting for transfers between devices: 7.68 us -> 6.84 us  [local(): pieces = lax.all_to_all(g, ('x', 'y'), 0, 0, tiled=True)]
    select_n x1 -> x0, other arithmetic: 0.69 us -> none  [local(): jnp.where(core == 0, jnp.stack([off_own, off_other]), jnp.stack([off_othe...]
    pallas_call x0 -> x1, Pallas kernels: none -> 0.68 us  [assemble(): pl.pallas_call(kernel, in_specs=[scalars(), whole(), whole()], out_specs=...]
  transfers between devices with their start and end apart: 7 -> 7, of which waited for: 3 -> 4; matrix products, arithmetic and copies ran while one was open for 1% -> 0% of each run, Pallas kernels for 9% -> 10%
where the time goes in v6:
time: 60.5 us; the launch traced here: 60.2 us
  starting transfers between devices  24.4 us (40%)
  waiting for transfers between devices  22.8 us (38%)
  Pallas kernels  11.6 us (19%)
  between operations  0.73 us (1%)
  local copies, waits for them, and re-layouts  0.69 us (1%)
    ppermute x1, waiting for transfers between devices, local(): arrived = lax.ppermute(sent, 'zl', xor4[1])  9.16 us
    all_to_all x1, starting transfers between devices, local(): pieces = lax.all_to_all(g, ('x', 'y'), 0, 0, tiled=True)  7.83 us
    all_to_all x1, starting transfers between devices, local(): pieces = lax.all_to_all(gathered, ('zh', 'zl', 'c'), 0, 0, tiled=True)  7.09 us
    all_to_all x1, waiting for transfers between devices, local(): pieces = lax.all_to_all(g, ('x', 'y'), 0, 0, tiled=True)  6.84 us
    all_to_all x1, waiting for transfers between devices, local(): pieces = lax.all_to_all(gathered, ('zh', 'zl', 'c'), 0, 0, tiled=True)  5.6 us
    pallas_call x2, Pallas kernels, product_rows(): pl.pallas_call(kernel, in_specs=[scalars(), whole(), hbm(), whole(), whol...  4.65 us
    pallas_call x1, Pallas kernels, product_sent(): pl.pallas_call(kernel, in_specs=[scalars(), hbm(), hbm(), hbm()], out_spe...  3.45 us
    ppermute x1, starting transfers between devices, local(): swapped = lax.ppermute(other, 'c', swap)  3.39 us
  transfers between devices with their start and end apart: 7, of which 4 were waited for; matrix products, arithmetic and copies ran while one was open for 0% of the time, Pallas kernels for 10%

profile of v6, /device:TPU:1, one launch (start us, length us, event | category | flops | bytes accessed | tf_op | source)
XLA Modules:
  0.0 60.2 jit_solution(9747660132480623028)
XLA Ops:
  0.6 0.0 copy-start
  0.7 0.7 %copy-done = s32[2,80]{1,0:T(2,128)S(1)} copy-done((s32[2,80]{1,0:T(2,128)S(1)}, s32[2,80]{1,0:T(2,128)}, u32[]{:S(2)}) %copy-start) | copy-done | bytes 664
  1.3 3.4 %product_sent.1 = (bf16[640,512]{1,0:T(8,128)(2,1)S(1)}, bf16[640,2560]{1,0:T(8,128)(2,1)S(1)}, bf16[320,512]{1,0:T(8,128)(2,1)S(1)}) custom-call(s32[1]{0:T(128)} %bitcast.me_ref, bf16[640,2560]{1,0:T(8,128)(2,1)} %a_hbm.1, bf16[2,2560,512]{2,1,0:T(8,128)(2,1)} %l_hbm.5, s32[2,80]{1,0:T(2,128)S(1)} %copy-done), custom_call_target="tpu_custom_call" | custom-call | flops 1677721600 | bytes 6553600 | tf_op jit(solution)/shard_map/product_sent/pallas_call | solution.py:122
  4.8 3.4 %collective-permute-start.1 = (bf16[640,512]{1,0:T(8,128)(2,1)S(1)}, bf16[640,512]{1,0:T(8,128)(2,1)S(1)}, u32[]{:S(2)}, u32[]{:S(2)}) collective-permute-start(bf16[640,512]{1,0:T(8,128)(2,1)S(1)} %get-tuple-element.14), channel_id=1, source_target_pairs={{0,1},{1,0},{2,3},{3,2},{4,5},{5,4},{6,7},{7,6},{8,9},{9,8},{10,11... | collective-permute-start | bytes 1966088 | tf_op jit(solution)/shard_map/ppermute | solution.py:332
  8.2 2.1 %collective-permute-start = (bf16[320,512]{1,0:T(8,128)(2,1)S(1)}, bf16[320,512]{1,0:T(8,128)(2,1)S(1)}, u32[]{:S(2)}, u32[]{:S(2)}) collective-permute-start(bf16[320,512]{1,0:T(8,128)(2,1)S(1)} %get-tuple-element.12), channel_id=1, source_target_pairs={{0,1},{1,36},{2,67},{3,100},{4,129},{5,167},{6,192},{7,225},{8,9},... | collective-permute-start | bytes 983048 | tf_op jit(solution)/shard_map/ppermute | solution.py:333
  10.3 0.0 collective-permute-done.1.in_ref
  10.3 2.3 %product_rows.3 = bf16[320,512]{1,0:T(8,128)(2,1)S(1)} custom-call(s32[1]{0:T(128)} %bitcast.me_ref, bf16[640,2560]{1,0:T(8,128)(2,1)S(1)} %get-tuple-element.13.a_ref, bf16[2,2560,512]{2,1,0:T(8,128)(2,1)} %l_hbm.5, s32[2,80]{1,0:T(2,128)S(1)} %copy-done, bf16[640,512]{1,0:T(8,128)(2,1)S(1)} %collective-permute-done.1.in_ref), custom_call_target="tpu_custom_call" | custom-call | flops 838860800 | bytes 4587520 | tf_op jit(solution)/shard_map/product_rows/pallas_call | solution.py:179
  12.6 0.0 copy-start.1
  12.6 1.6 %collective-permute-start.2 = (bf16[320,512]{1,0:T(8,128)(2,1)S(1)}, bf16[320,512]{1,0:T(8,128)(2,1)S(1)}, u32[]{:S(2)}, u32[]{:S(2)}) collective-permute-start(bf16[320,512]{1,0:T(8,128)(2,1)S(1)} %product_rows.3), channel_id=1, source_target_pairs={{0,2},{2,0},{4,6},{6,4},{1,3},{3,1},{5,7},{7,5},{8,10},{10,8},{12,... | collective-permute-start | bytes 983048 | tf_op jit(solution)/shard_map/ppermute | solution.py:335
  14.3 2.3 %product_rows.2 = (f32[160,512]{1,0:T(8,128)S(1)}, f32[160,512]{1,0:T(8,128)S(1)}) custom-call(s32[1]{0:T(128)} %bitcast.me_ref, bf16[640,2560]{1,0:T(8,128)(2,1)S(1)} %get-tuple-element.13.a_ref, bf16[2,2560,512]{2,1,0:T(8,128)(2,1)} %l_hbm.5, s32[2,80]{1,0:T(2,128)S(1)} %copy-done, bf16[640,512]{1,0:T(8,128)(2,1)S(1)} %collective-permute-done.1.in_ref), custom_call_target="tpu_custom_call" | custom-call | flops 838860800 | bytes 4587520 | tf_op jit(solution)/shard_map/product_rows/pallas_call | solution.py:179
  16.6 0.0 copy-start.2
  16.6 9.2 %collective-permute-done.2.in_ref = bf16[320,512]{1,0:T(8,128)(2,1)S(1)} collective-permute-done((bf16[320,512]{1,0:T(8,128)(2,1)S(1)}, bf16[320,512]{1,0:T(8,128)(2,1)S(1)}, u32[]{:S(2)}, u32[]{:S(2)}) %collective-permute-start.2) | collective-permute-done | bytes 327712 | tf_op jit(solution)/shard_map/ppermute | solution.py:335
  25.8 1.4 %contract.1 = (f32[160,512]{1,0:T(8,128)S(1)}, bf16[160,512]{1,0:T(8,128)(2,1)S(1)}, bf16[16,32,512]{2,1,0:T(8,128)(2,1)}) custom-call(s32[1]{0:T(128)} %bitcast.me_ref, s32[2,80]{1,0:T(2,128)S(1)} %copy-done, bf16[320,512]{1,0:T(8,128)(2,1)S(1)} %collective-permute-done.m_ref, f32[160,512]{1,0:T(8,128)S(1)} %get-tuple-element.15.near_ref, ...), custom_call_target="tpu_custom_call" | custom-call | tf_op jit(solution)/shard_map/contract/pallas_call | solution.py:225
  27.1 7.8 %all-to-all-start = ((bf16[16,32,512]{2,1,0:T(8,128)(2,1)}), bf16[16,32,512]{2,1,0:T(8,128)(2,1)S(1)}, u32[]{:S(2)}, u32[]{:S(2)}) async-start(bf16[16,32,512]{2,1,0:T(8,128)(2,1)} %get-tuple-element.19), calls=%async_computation | async-start | bytes 1048576 | tf_op jit(solution)/shard_map/all_to_all | solution.py:339
  35.0 2.2 %collective-permute-start.3 = (bf16[160,512]{1,0:T(8,128)(2,1)S(1)}, bf16[160,512]{1,0:T(8,128)(2,1)S(1)}, u32[]{:S(2)}, u32[]{:S(2)}) collective-permute-start(bf16[160,512]{1,0:T(8,128)(2,1)S(1)} %get-tuple-element.18), channel_id=1, source_target_pairs={{0,4},{2,6},{4,0},{6,2},{1,5},{3,7},{5,1},{7,3},{8,12},{10,14},{12... | collective-permute-start | bytes 491528 | tf_op jit(solution)/shard_map/ppermute | solution.py:338
  37.2 6.8 %all-to-all-done.in_ref = bf16[16,32,512]{2,1,0:T(8,128)(2,1)S(1)} async-done(((bf16[16,32,512]{2,1,0:T(8,128)(2,1)}), bf16[16,32,512]{2,1,0:T(8,128)(2,1)S(1)}, u32[]{:S(2)}, u32[]{:S(2)}) %all-to-all-start) | async-done | bytes 524320 | tf_op jit(solution)/shard_map/all_to_all | solution.py:339
  44.0 0.7 %gather.1.after_ref = f32[16,2,512]{2,1,0:T(2,128)} custom-call(bf16[16,32,512]{2,1,0:T(8,128)(2,1)S(1)} %all-to-all-done.in_ref), custom_call_target="tpu_custom_call" | custom-call | tf_op jit(solution)/shard_map/gather/pallas_call | solution.py:290
  44.7 7.1 %all-to-all-start.1 = ((f32[16,2,512]{2,1,0:T(2,128)}), f32[16,2,512]{2,1,0:T(2,128)S(1)}, u32[]{:S(2)}, u32[]{:S(2)}) async-start(f32[16,2,512]{2,1,0:T(2,128)} %gather.1.after_ref), calls=%async_computation.1 | async-start | bytes 131072 | tf_op jit(solution)/shard_map/all_to_all | solution.py:344
  51.8 0.1 negate.1
  52.0 0.2 collective-permute-start.4
  52.2 1.2 %collective-permute-done.4.other_ref = bf16[80,512]{1,0:T(8,128)(2,1)S(1)} collective-permute-done((bf16[80,512]{1,0:T(8,128)(2,1)S(1)}, bf16[80,512]{1,0:T(8,128)(2,1)S(1)}, u32[]{:S(2)}, u32[]{:S(2)}) %collective-permute-start.4) | collective-permute-done | bytes 81952 | tf_op jit(solution)/shard_map/ppermute | solution.py:342
  53.3 0.7 %assemble.1 = bf16[2,80,512]{2,1,0:T(8,128)(2,1)} custom-call(s32[1]{0:T(128)} %bitcast.me_ref, bf16[80,512]{1,0:T(8,128)(2,1)S(1)} %get-tuple-element.20.own_ref, bf16[80,512]{1,0:T(8,128)(2,1)S(1)} %collective-permute-done.4.other_ref), custom_call_target="tpu_custom_call" | custom-call | flops 1 | bytes 1 | tf_op jit(solution)/shard_map/assemble/pallas_call | solution.py:269
  54.0 5.6 %all-to-all-done.1.in_ref = f32[16,2,512]{2,1,0:T(2,128)S(1)} async-done(((f32[16,2,512]{2,1,0:T(2,128)}), f32[16,2,512]{2,1,0:T(2,128)S(1)}, u32[]{:S(2)}, u32[]{:S(2)}) %all-to-all-start.1) | async-done | bytes 65568 | tf_op jit(solution)/shard_map/all_to_all | solution.py:344
  59.6 0.6 %finish.1 = f32[2,2,512]{2,1,0:T(2,128)} custom-call(f32[16,2,512]{2,1,0:T(2,128)S(1)} %all-to-all-done.1.in_ref, f32[2,2,512]{2,1,0:T(2,128)S(1)} %copy-done.2), custom_call_target="tpu_custom_call" | custom-call | tf_op jit(solution)/shard_map/finish/pallas_call | solution.py:308
  (4 shorter events, 0.0 us)
Async XLA Ops:
  0.6 0.7 %copy-start = (s32[2,80]{1,0:T(2,128)S(1)}, s32[2,80]{1,0:T(2,128)}, u32[]{:S(2)}) copy-start(s32[2,80]{1,0:T(2,128)} %p_ref.7) | copy-start | bytes 1924
  4.8 5.5 %collective-permute-start.1 = (bf16[640,512]{1,0:T(8,128)(2,1)S(1)}, bf16[640,512]{1,0:T(8,128)(2,1)S(1)}, u32[]{:S(2)}, u32[]{:S(2)}) collective-permute-start(bf16[640,512]{1,0:T(8,128)(2,1)S(1)} %get-tuple-element.14), channel_id=1, source_target_pairs={{0,1},{1,0},{2,3},{3,2},{4,5},{5,4},{6,7},{7,6},{8,9},{9,8},{10,11... | collective-permute-start | bytes 1966088 | tf_op jit(solution)/shard_map/ppermute | solution.py:332
  8.2 8.4 %collective-permute-start = (bf16[320,512]{1,0:T(8,128)(2,1)S(1)}, bf16[320,512]{1,0:T(8,128)(2,1)S(1)}, u32[]{:S(2)}, u32[]{:S(2)}) collective-permute-start(bf16[320,512]{1,0:T(8,128)(2,1)S(1)} %get-tuple-element.12), channel_id=1, source_target_pairs={{0,1},{1,36},{2,67},{3,100},{4,129},{5,167},{6,192},{7,225},{8,9},... | collective-permute-start | bytes 983048 | tf_op jit(solution)/shard_map/ppermute | solution.py:333
  12.6 39.2 %copy-start.1 = (s32[2,80]{1,0:T(2,128)S(1)}, s32[2,80]{1,0:T(2,128)}, u32[]{:S(2)}) copy-start(s32[2,80]{1,0:T(2,128)} %p_ref.7) | copy-start | bytes 1924
  12.6 13.1 %collective-permute-start.2 = (bf16[320,512]{1,0:T(8,128)(2,1)S(1)}, bf16[320,512]{1,0:T(8,128)(2,1)S(1)}, u32[]{:S(2)}, u32[]{:S(2)}) collective-permute-start(bf16[320,512]{1,0:T(8,128)(2,1)S(1)} %product_rows.3), channel_id=1, source_target_pairs={{0,2},{2,0},{4,6},{6,4},{1,3},{3,1},{5,7},{7,5},{8,10},{10,8},{12,... | collective-permute-start | bytes 983048 | tf_op jit(solution)/shard_map/ppermute | solution.py:335
  16.6 43.0 %copy-start.2 = (f32[2,2,512]{2,1,0:T(2,128)S(1)}, f32[2,2,512]{2,1,0:T(2,128)}, u32[]{:S(2)}) copy-start(f32[2,2,512]{2,1,0:T(2,128)} %d_ref.1) | copy-start | bytes 24580
  27.1 16.9 %all-to-all-start = ((bf16[16,32,512]{2,1,0:T(8,128)(2,1)}), bf16[16,32,512]{2,1,0:T(8,128)(2,1)S(1)}, u32[]{:S(2)}, u32[]{:S(2)}) async-start(bf16[16,32,512]{2,1,0:T(8,128)(2,1)} %get-tuple-element.19), calls=%async_computation | async-start | bytes 1048576 | tf_op jit(solution)/shard_map/all_to_all | solution.py:339
  35.0 16.8 %collective-permute-start.3 = (bf16[160,512]{1,0:T(8,128)(2,1)S(1)}, bf16[160,512]{1,0:T(8,128)(2,1)S(1)}, u32[]{:S(2)}, u32[]{:S(2)}) collective-permute-start(bf16[160,512]{1,0:T(8,128)(2,1)S(1)} %get-tuple-element.18), channel_id=1, source_target_pairs={{0,4},{2,6},{4,0},{6,2},{1,5},{3,7},{5,1},{7,3},{8,12},{10,14},{12... | collective-permute-start | bytes 491528 | tf_op jit(solution)/shard_map/ppermute | solution.py:338
  44.7 14.9 %all-to-all-start.1 = ((f32[16,2,512]{2,1,0:T(2,128)}), f32[16,2,512]{2,1,0:T(2,128)S(1)}, u32[]{:S(2)}, u32[]{:S(2)}) async-start(f32[16,2,512]{2,1,0:T(2,128)} %gather.1.after_ref), calls=%async_computation.1 | async-start | bytes 131072 | tf_op jit(solution)/shard_map/all_to_all | solution.py:344
  52.0 1.4 %collective-permute-start.4 = (bf16[80,512]{1,0:T(8,128)(2,1)S(1)}, bf16[80,512]{1,0:T(8,128)(2,1)S(1)}, u32[]{:S(2)}, u32[]{:S(2)}) collective-permute-start(bf16[80,512]{1,0:T(8,128)(2,1)S(1)} %get-tuple-element.21), channel_id=1, source_target_pairs={{0,1},{1,0},{2,3},{3,2},{4,5},{5,4},{6,7},{7,6},{8,9},{9,8},{10,11... | collective-permute-start | bytes 245768 | tf_op jit(solution)/shard_map/ppermute | solution.py:342
